TPU v7x, 128 devices: a whole 4x4x4 slice. The times are simulated.
128 devices in a mesh: section: 8 (over y, x_hi), seq: 16 (over x_lo, z, core).
Axes of the slice: x: 4 (x_hi: 2, x_lo: 2; x = x_hi * 2 + x_lo), y: 4, z: 4, core: 2. Of those that a mesh axis runs over, the one named last changes fastest.
Arguments:
- teacher_query_array: bfloat16 [8, 4096, 4096], P('section', 'seq'), may hold values from -8 to 8
- teacher_keys: bfloat16 [8, 4096, 512], P('section', 'seq'), may hold values from -8 to 8
- teacher_value_array: bfloat16 [8, 4096, 512], P('section', 'seq'), may hold values from -6 to 6
- projection: bfloat16 [8, 8, 512, 128], P('section'), may hold values from -0.25 to 0.25
- student_query_array: bfloat16 [8, 2048, 2048], P('section', 'seq'), may hold values from -8 to 8
- student_keys: bfloat16 [8, 2048, 512], P('section', 'seq'), may hold values from -8 to 8
- student_value_array: bfloat16 [8, 2048, 512], P('section', 'seq'), may hold values from -6 to 6
Outputs:
- grad_student_q: float32 [8, 2048, 2048], P('section', 'seq')
- grad_student_keys: float32 [8, 2048, 512], P('section', 'seq')
- grad_student_values: float32 [8, 2048, 512], P('section', 'seq')
- per_token_loss: float32 [8, 2048], P('section', 'seq')
All inputs are finite; a program needn't handle non-finite values.
Results may differ from a plain program's by a relative error of at most 0.03.
Values may be sent and summed in bfloat16 or wider, within the bound.
A program may use at most 128 MiB of HBM per device.

v0:
```python
import math

import jax
import jax.numpy as jnp
from jax import lax
from jax.sharding import PartitionSpec as P

HEAD_SIZE = 128
TEACHER_Q_HEADS = 64
TEACHER_KV_HEADS = 8
STUDENT_Q_HEADS = 16
STUDENT_KV_HEADS = 4


floor_score = -1e30


def sent_together(arrays, axis, dim, along):
    ends, at = ([], 0)
    for a in arrays[:-1]:
        at += a.shape[along]
        ends.append(at)
    both = jnp.concatenate(arrays, axis=along)
    return tuple(jnp.split(lax.all_gather(both, axis, axis=dim, tiled=True), ends, axis=along))


def partner(value, axis, apart):
    mask = 2**apart
    pairs = [(source, source ^ mask) for source in range(lax.axis_size(axis))]
    return lax.ppermute(value, axis, pairs)


def blocking(row_count):
    return math.gcd(row_count, 512)


def absorb(carried, key_block, value_block, block_start, queries, query_pos):
    row_peak, row_total, weighted = carried
    inverse_root = 1.0 / math.sqrt(queries.shape[3])
    scores = (
        jnp.einsum("qgjd,kgd->gjqk", queries, key_block, preferred_element_type=jnp.float32)
        * inverse_root
    )
    key_pos = block_start + jnp.arange(key_block.shape[0], dtype=jnp.int32)
    allowed = key_pos[None, None, None, :] <= query_pos[None, None, :, None]
    scores = jnp.where(allowed, scores, floor_score)
    new_peak = jnp.maximum(row_peak, jnp.max(scores, axis=-1))
    rescale = jnp.exp(row_peak - new_peak)
    weights = jnp.where(allowed, jnp.exp(scores - new_peak[..., None]), 0.0)
    row_total = row_total * rescale + jnp.sum(weights, axis=-1)
    weighted = weighted * jnp.transpose(rescale, (2, 0, 1))[..., None] + jnp.einsum(
        "gjqk,kgd->qgjd",
        weights.astype(jnp.bfloat16),
        value_block,
        preferred_element_type=jnp.float32,
    )
    return (new_peak, row_total, weighted)


def online_pass(carried, key_rows, value_rows, queries, query_pos):
    row_count = key_rows.shape[0]
    rows_per_block = blocking(row_count)
    count_of_blocks = row_count // rows_per_block
    heads_of_keys = queries.shape[1]
    head_width = queries.shape[3]
    blocked_keys = key_rows.reshape(count_of_blocks, rows_per_block, heads_of_keys, head_width)
    blocked_values = value_rows.reshape(count_of_blocks, rows_per_block, heads_of_keys, head_width)
    last_query = query_pos[-1]

    def online_step(status, element):
        block_index, key_block, value_block = element
        block_start = block_index * rows_per_block
        status = lax.cond(
            block_start <= last_query,
            lambda current: absorb(
                current, key_block, value_block, block_start, queries, query_pos
            ),
            lambda current: current,
            status,
        )
        return (status, None)

    status, _ = lax.scan(
        online_step,
        carried,
        (jnp.arange(count_of_blocks, dtype=jnp.int32), blocked_keys, blocked_values),
    )
    return status


def fresh_state(queries):
    row_shape = (queries.shape[1], queries.shape[2], queries.shape[0])
    return (
        jnp.full(row_shape, floor_score, jnp.float32),
        jnp.zeros(row_shape, jnp.float32),
        jnp.zeros(queries.shape, jnp.float32),
    )


def finish(status):
    row_peak, row_total, weighted = status
    return weighted / jnp.transpose(row_total, (2, 0, 1))[..., None]


def body(
    teacher_query_array,
    teacher_keys,
    teacher_value_array,
    projection,
    student_query_array,
    student_keys,
    student_value_array,
):
    section_index = lax.axis_index("section")
    pair_bit = section_index % 2
    seq_index = lax.axis_index("seq")
    rows_of_teacher = teacher_query_array.shape[1]
    queries_of_teacher = teacher_query_array[0].reshape(
        rows_of_teacher, TEACHER_KV_HEADS // 2, TEACHER_Q_HEADS // TEACHER_KV_HEADS, HEAD_SIZE
    )
    teacher_pos = seq_index * rows_of_teacher + jnp.arange(rows_of_teacher, dtype=jnp.int32)
    portion = sent_together((teacher_keys[0], teacher_value_array[0]), "seq", 0, 1)
    status = online_pass(
        fresh_state(queries_of_teacher), portion[0], portion[1], queries_of_teacher, teacher_pos
    )
    context = (
        finish(status)
        .astype(jnp.bfloat16)
        .reshape(
            rows_of_teacher, STUDENT_Q_HEADS // 2, TEACHER_Q_HEADS // STUDENT_Q_HEADS * HEAD_SIZE
        )
    )
    target = jnp.einsum(
        "thf,hfe->the", context, projection[0], preferred_element_type=jnp.float32
    ).astype(jnp.bfloat16)
    rows_of_student = rows_of_teacher // 2
    own_target = lax.dynamic_slice_in_dim(target, pair_bit * rows_of_student, rows_of_student, 0)
    other_target = lax.dynamic_slice_in_dim(
        target, (1 - pair_bit) * rows_of_student, rows_of_student, 0
    )
    other_target = partner(other_target, "section", 0)
    rows_of_target = jnp.where(
        pair_bit == 0,
        jnp.concatenate([own_target, other_target], 1),
        jnp.concatenate([other_target, own_target], 1),
    )
    rows_of_target = rows_of_target.reshape(
        rows_of_student, STUDENT_KV_HEADS, STUDENT_Q_HEADS // STUDENT_KV_HEADS, HEAD_SIZE
    )
    own_keys = student_keys[0]
    own_values = student_value_array[0]
    far_keys, far_values = partner((own_keys, own_values), "section", 0)
    block_keys = jnp.where(
        pair_bit == 0,
        jnp.concatenate([own_keys, far_keys], 0),
        jnp.concatenate([far_keys, own_keys], 0),
    )
    block_values = jnp.where(
        pair_bit == 0,
        jnp.concatenate([own_values, far_values], 0),
        jnp.concatenate([far_values, own_values], 0),
    )
    every_key, every_value = (
        lax.all_gather(block_keys, "seq", axis=0, tiled=True),
        lax.all_gather(block_values, "seq", axis=0, tiled=True),
    )
    queries_of_student = student_query_array[0].reshape(
        rows_of_student, STUDENT_KV_HEADS, STUDENT_Q_HEADS // STUDENT_KV_HEADS, HEAD_SIZE
    )
    student_pos = (
        seq_index * 2 * rows_of_student
        + pair_bit * rows_of_student
        + jnp.arange(rows_of_student, dtype=jnp.int32)
    )
    status = online_pass(
        fresh_state(queries_of_student), every_key, every_value, queries_of_student, student_pos
    )
    row_peak, row_total, weighted = status
    student_context = finish(status)
    mismatch = student_context - rows_of_target.astype(jnp.float32)
    per_token_loss = jnp.mean(jnp.square(mismatch).reshape(rows_of_student, -1), axis=1)
    grad_context = mismatch.astype(jnp.bfloat16)
    row_delta = jnp.transpose(jnp.sum(mismatch * student_context, axis=-1), (1, 2, 0))
    row_total_count = every_key.shape[0]
    rows_per_block = blocking(row_total_count)
    count_of_blocks = row_total_count // rows_per_block
    blocked_keys = every_key.reshape(count_of_blocks, rows_per_block, STUDENT_KV_HEADS, HEAD_SIZE)
    blocked_values = every_value.reshape(
        count_of_blocks, rows_per_block, STUDENT_KV_HEADS, HEAD_SIZE
    )
    inverse_root = 1.0 / math.sqrt(HEAD_SIZE)
    last_query = student_pos[-1]

    def backward_step(query_gradient, element):
        block_index, key_block, value_block = element
        block_start = block_index * rows_per_block

        def active_block(query_gradient):
            key_pos = block_start + jnp.arange(rows_per_block, dtype=jnp.int32)
            allowed = key_pos[None, None, None, :] <= student_pos[None, None, :, None]
            scores = (
                jnp.einsum(
                    "qgjd,kgd->gjqk",
                    queries_of_student,
                    key_block,
                    preferred_element_type=jnp.float32,
                )
                * inverse_root
            )
            probability = jnp.where(
                allowed, jnp.exp(scores - row_peak[..., None]) / row_total[..., None], 0.0
            )
            grad_prob = jnp.einsum(
                "qgjd,kgd->gjqk", grad_context, value_block, preferred_element_type=jnp.float32
            )
            grad_score = (probability * (grad_prob - row_delta[..., None])).astype(jnp.bfloat16)
            query_gradient = query_gradient + jnp.einsum(
                "gjqk,kgd->qgjd", grad_score, key_block, preferred_element_type=jnp.float32
            )
            grad_key = (
                jnp.einsum(
                    "gjqk,qgjd->kgd",
                    grad_score,
                    queries_of_student,
                    preferred_element_type=jnp.float32,
                )
                * inverse_root
            )
            grad_value = jnp.einsum(
                "gjqk,qgjd->kgd",
                probability.astype(jnp.bfloat16),
                grad_context,
                preferred_element_type=jnp.float32,
            )
            return (
                query_gradient,
                jnp.concatenate(
                    [grad_key.reshape(rows_per_block, -1), grad_value.reshape(rows_per_block, -1)],
                    1,
                ),
            )

        def skipped_block(query_gradient):
            return (
                query_gradient,
                jnp.zeros((rows_per_block, 2 * STUDENT_KV_HEADS * HEAD_SIZE), jnp.float32),
            )

        return lax.cond(block_start <= last_query, active_block, skipped_block, query_gradient)

    query_gradient, terms_of_keys = lax.scan(
        backward_step,
        jnp.zeros(queries_of_student.shape, jnp.float32),
        (jnp.arange(count_of_blocks, dtype=jnp.int32), blocked_keys, blocked_values),
    )
    terms_of_keys = terms_of_keys.reshape(row_total_count, 2 * STUDENT_KV_HEADS * HEAD_SIZE)
    query_gradient = (query_gradient * inverse_root).reshape(
        rows_of_student, STUDENT_Q_HEADS * HEAD_SIZE
    )
    summed = lax.psum_scatter(
        terms_of_keys.astype(jnp.bfloat16), "seq", scatter_dimension=0, tiled=True
    ).astype(jnp.float32)
    own_part = lax.dynamic_slice_in_dim(summed, pair_bit * rows_of_student, rows_of_student, 0)
    far_part = lax.dynamic_slice_in_dim(
        summed, (1 - pair_bit) * rows_of_student, rows_of_student, 0
    )
    key_grads = own_part + partner(far_part.astype(jnp.bfloat16), "section", 0).astype(
        far_part.dtype
    )
    width_of_keys = STUDENT_KV_HEADS * HEAD_SIZE
    return (
        query_gradient[None],
        key_grads[:, :width_of_keys][None],
        key_grads[:, width_of_keys:][None],
        per_token_loss[None],
    )


def solution(mesh):
    in_specs = (
        P("section", "seq", None),
        P("section", "seq", None),
        P("section", "seq", None),
        P("section", None, None, None),
        P("section", "seq", None),
        P("section", "seq", None),
        P("section", "seq", None),
    )
    out_specs = (
        P("section", "seq", None),
        P("section", "seq", None),
        P("section", "seq", None),
        P("section", "seq"),
    )
    return jax.shard_map(body, mesh=mesh, in_specs=in_specs, out_specs=out_specs, check_vma=False)
```

profile of v0, /device:TPU:1, one launch (start us, length us, event | category | flops | bytes accessed | tf_op | source)
XLA Modules:
  0.0 552.4 jit_solution(10814579748246716568)
XLA Ops:
  9.3 3.7 collective-permute-start.1
  12.9 3.0 collective-permute-done.1
  17.7 3.2 collective-permute-start
  20.9 2.6 collective-permute-done
  25.9 3.3 copy.39
  29.2 2.4 copy.42
  31.6 35.5 %all-gather.8.cloned.1.call-done = bf16[4096,1024]{1,0:T(8,128)(2,1)} async-done(((bf16[256,1024]{1,0:T(8,128)(2,1)}), bf16[4096,1024]{1,0:T(8,128)(2,1)}) %all-gather.8.cloned.1.call-update) | async-done | bytes 8388624 | tf_op jit(solution)/shard_map/all_gather | solution.py:24
  67.2 5.7 %fusion.68 = (bf16[4096,512]{1,0:T(8,128)(2,1)}, bf16[4096,512]{1,0:T(8,128)(2,1)}) fusion(bf16[4096,1024]{1,0:T(8,128)(2,1)} %all-gather.8.cloned.1.call-done), kind=kLoop, calls=%fused_computation.101 | loop fusion | bytes 16777216 | tf_op jit(solution)/shard_map/split | solution.py:24
  72.9 7.0 %reshape.193 = bf16[8,512,4,128]{3,2,1,0:T(4,128)(2,1)} reshape(bf16[4096,512]{1,0:T(8,128)(2,1)} %get-tuple-element.658) | data formatting | bytes 8388608 | tf_op jit(solution)/shard_map/reshape | solution.py:66
  79.9 5.2 copy.41
  85.0 7.1 %reshape.194 = bf16[8,512,4,128]{3,2,1,0:T(4,128)(2,1)} reshape(bf16[4096,512]{1,0:T(8,128)(2,1)} %get-tuple-element.657) | data formatting | bytes 8388608 | tf_op jit(solution)/shard_map/reshape | solution.py:67
  92.1 5.3 copy.43
  97.4 2.4 broadcast_in_dim.118
  99.9 32.0 %while.47 = (s32[]{:T(128)}, f32[4,8,256]{2,1,0:T(8,128)S(1)}, f32[4,8,256]{2,1,0:T(8,128)S(1)}, f32[256,4,8,128]{3,0,2,1:T(8,128)}, s32[8]{0:T(128)S(1)}, /*ind...) while((s32[]{:T(128)}, f32[4,8,256]{2,1,0:T(8,128)S(1)}, ...), condition=%wide.region_11.12_spmd.clone, body=%wide.region_6.11_spmd.clone.sunk | while | flops 2204263168 | bytes 62924072 | solution.py:83
  101.7 17.2 %conditional.10 = ((f32[4,8,256]{2,1,0:T(8,128)S(1)}, f32[4,8,256]{2,1,0:T(8,128)S(1)}, f32[256,4,8,128]{3,0,2,1:T(8,128)})) conditional(s32[]{:T(128)} %convert_element_type.96, (f32[4,8,256]{2,1,0:T(8,128)S(1)}, f32[4,8,256]{2,1,0:T(8,128)S(1)}, f32[256,4,8,128]{3,0,2,1:T(8,128)}) %tuple.117, (s32[]{:T(128)}, s32[]{:T(128)}, ...), branch_computations={%region_7.7_spmd, %region_8.10_spmd} | conditional | flops 2204263168 | bytes 62922792 | solution.py:73
  101.9 4.2 fusion.29
  106.0 4.2 fusion.31
  110.3 8.6 %bitcast_add_fusion = f32[256,4,8,128]{3,0,2,1:T(8,128)} fusion(f32[256,4,8,128]{3,0,2,1:T(8,128)} %get-tuple-element.383, f32[4,512,256,8]{2,1,3,0:T(8,128)S(1)} %get-tuple-element.656, f32[4,8,256]{2,1,0:T(8,128)S(1)} %get-tuple-element.889, pred[256,512]{0,1:T(8,128)(4,1)S(1)} %broadcast_compare_fusion.1, f32[256,4,8]{0,2,1:T(8,128)S(1)} %get-tuple-element.649, ...), kind=kOutput, calls=%fused_computation.35 | convolution fusion | flops 1096810496 | bytes 25887232 | tf_op jit(solution)/shard_map/while/body/eval_jaxpr/cond/branch_1_fun/gjqk,kgd->qgjd/dot_general | solution.py:51
  131.8 5.4 copy.44
  137.3 2.9 divide_convert_fusion
  146.2 6.9 %reshape.192 = bf16[8,512,4,128]{3,2,1,0:T(4,128)(2,1)} reshape(bf16[4096,512]{1,0:T(8,128)(2,1)} %all-gather.6.cloned.1.call-done) | data formatting | bytes 8388608 | tf_op jit(solution)/shard_map/reshape | solution.py:188
  153.1 5.1 copy.36
  158.3 6.9 %reshape.191 = bf16[8,512,4,128]{3,2,1,0:T(4,128)(2,1)} reshape(bf16[4096,512]{1,0:T(8,128)(2,1)} %all-gather.4.cloned.1.call-done) | data formatting | bytes 8388608 | tf_op jit(solution)/shard_map/reshape | solution.py:187
  165.2 5.2 copy.47
  170.5 21.1 %while.46 = (s32[]{:T(128)}, f32[4,4,128]{2,1,0:T(4,128)S(1)}, f32[4,4,128]{2,1,0:T(4,128)S(1)}, f32[128,4,4,128]{3,0,2,1:T(8,128)S(1)}, s32[8]{0:T(128)S(1)}, /...) while((s32[]{:T(128)}, f32[4,4,128]{2,1,0:T(4,128)S(1)}, ...), condition=%wide.region_5.6_spmd.clone, body=%wide.region_0.5_spmd.clone.sunk | while | flops 551099008 | bytes 16653611 | solution.py:83
  172.4 5.8 %conditional.9 = ((f32[4,4,128]{2,1,0:T(4,128)S(1)}, f32[4,4,128]{2,1,0:T(4,128)S(1)}, f32[128,4,4,128]{3,0,2,1:T(8,128)S(1)})) conditional(s32[]{:T(128)} %convert_element_type.95, (f32[4,4,128]{2,1,0:T(4,128)S(1)}, f32[4,4,128]{2,1,0:T(4,128)S(1)}, f32[128,4,4,128]{3,0,2,1:T(8,128)S(1)}) %tuple.114, (s32[]{:T(128)}, s32[]{:T(128)}, ...), branch_computations={%region_1.1_spmd, %region_2.4_spmd} | conditional | flops 551099008 | bytes 16652840 | solution.py:73
  175.4 2.7 fusion.15
  194.5 33.5 %while.48 = (s32[]{:T(128)}, f32[128,4,4,128]{3,0,2,1:T(8,128)S(1)}, bf16[8,512,1024]{1,2,0:T(8,128)(2,1)}, s32[8]{0:T(128)S(1)}, s32[]{:T(128)}, /*index=5*/bf1...) while((s32[]{:T(128)}, ...), condition=%wide.region_16.17_spmd.clone, body=%wide.region_13.16_spmd.clone.sunk | while | flops 1353515648 | bytes 30048556 | solution.py:251
  196.4 9.3 %conditional.11 = (f32[128,4,4,128]{3,0,2,1:T(8,128)S(1)}, bf16[1,512,1024]{1,2,0:T(8,128)(2,1)S(1)}) conditional(s32[]{:T(128)} %convert_element_type.97, f32[128,4,4,128]{3,0,2,1:T(8,128)S(1)} %get-tuple-element.984, (s32[]{:T(128)}, s32[]{:T(128)}, bf16[8,512,4,128]{3,1,2,0:T(8,128)(2,1)}, s32[]{:T(128)}, bf16[128,4,4,128]{0,3,2,1:T(8,128)(2,1)}, ...), branch_computations={%region_14.14_spmd, %region_15.15_spmd} | conditional | flops 1353515648 | bytes 27950104 | solution.py:249
  203.3 2.3 fusion.55
  228.0 11.5 %copy.50 = bf16[8,512,1024]{2,1,0:T(8,128)(2,1)} copy(bf16[8,512,1024]{1,2,0:T(8,128)(2,1)} %get-tuple-element.443) | data formatting | bytes 16777216 | tf_op jit(solution)/shard_map/convert_element_type | solution.py:261
  239.5 296.7 %reduce-scatter.2.cloned.1.call-done = bf16[256,1024]{1,0:T(8,128)(2,1)} async-done(((bf16[4096,1024]{1,0:T(8,128)(2,1)}), bf16[256,1024]{1,0:T(8,128)(2,1)}) %reduce-scatter.2.cloned.1.call-update) | async-done | bytes 524304 | tf_op jit(solution)/shard_map/reduce_scatter | solution.py:260
  (160 shorter events, 59.1 us)
Async XLA Ops:
  7.2 133.0 %copy-start = (bf16[1,8,512,128]{3,2,1,0:T(8,128)(2,1)S(1)}, bf16[1,8,512,128]{3,2,1,0:T(8,128)(2,1)}, u32[]{:S(2)}) copy-start(bf16[1,8,512,128]{3,2,1,0:T(8,128)(2,1)} %param.22) | copy-start | bytes 3145732
  7.2 60.0 %all-gather.8.cloned.1.call-start = ((), (), s32[]{:S(2)}) async-start(), calls=%async_computation.3 | async-start | bytes 8912896 | tf_op jit(solution)/shard_map/all_gather | solution.py:24
  9.2 137.0 %all-gather.6.cloned.1.call-start = ((), (), s32[]{:S(2)}) async-start(), calls=%async_computation.2 | async-start | bytes 4456448 | tf_op jit(solution)/shard_map/all_gather | solution.py:165
  9.3 6.6 %collective-permute-start.1 = (bf16[128,512]{1,0:T(8,128)(2,1)}, bf16[128,512]{1,0:T(8,128)(2,1)S(1)}, u32[]{:S(2)}, u32[]{:S(2)}) collective-permute-start(bf16[128,512]{1,0:T(8,128)(2,1)} %bitcast.183), channel_id=1, source_target_pairs={{0,16},{16,0},{32,48},{48,32},{64,80},{80,64},{96,112},{112,96},{1... | collective-permute-start | bytes 393224 | tf_op jit(solution)/shard_map/ppermute | solution.py:30
  17.6 140.6 %all-gather.4.cloned.1.call-start = ((), (), s32[]{:S(2)}) async-start(), calls=%async_computation.1 | async-start | bytes 4456448 | tf_op jit(solution)/shard_map/all_gather | solution.py:164
  17.7 5.8 %collective-permute-start = (bf16[128,512]{1,0:T(8,128)(2,1)}, bf16[128,512]{1,0:T(8,128)(2,1)S(1)}, u32[]{:S(2)}, u32[]{:S(2)}) collective-permute-start(bf16[128,512]{1,0:T(8,128)(2,1)} %bitcast.185), channel_id=1, source_target_pairs={{0,16},{16,0},{32,48},{48,32},{64,80},{80,64},{96,112},{112,96},{1... | collective-permute-start | bytes 393224 | tf_op jit(solution)/shard_map/ppermute | solution.py:30
  25.2 510.9 %reduce-scatter.2.cloned.1.call-start = ((), (), s32[]{:S(2)}) async-start(), calls=%async_computation.4 | async-start | bytes 8912896 | tf_op jit(solution)/shard_map/reduce_scatter | solution.py:260
  137.3 6.6 %copy-start.2 = (bf16[1,128,2048]{2,1,0:T(8,128)(2,1)S(1)}, bf16[1,128,2048]{2,1,0:T(8,128)(2,1)}, u32[]{:S(2)}) copy-start(bf16[1,128,2048]{2,1,0:T(8,128)(2,1)} %param.23) | copy-start | bytes 1572868
  141.5 50.5 %collective-permute-start.2 = (bf16[128,8,128]{0,2,1:T(8,128)(2,1)}, bf16[128,8,128]{0,2,1:T(8,128)(2,1)S(1)}, u32[]{:S(2)}, u32[]{:S(2)}) collective-permute-start(bf16[128,8,128]{0,2,1:T(8,128)(2,1)} %get-tuple-element.661), channel_id=1, source_target_pairs={{0,16},{16,0},{32,48},{48,32},{64,80},{80,64},{96,112},{112,96},{1... | collective-permute-start | bytes 786440 | tf_op jit(solution)/shard_map/ppermute | solution.py:30
  191.9 0.7 copy-start.3
  538.1 6.9 %collective-permute-start.3 = (bf16[128,1024]{1,0:T(8,128)(2,1)}, bf16[128,1024]{1,0:T(8,128)(2,1)S(1)}, u32[]{:S(2)}, u32[]{:S(2)}) collective-permute-start(bf16[128,1024]{1,0:T(8,128)(2,1)} %dynamic-slice_convert_fusion), channel_id=1, source_target_pairs={{0,16},{16,0},{32,48},{48,32},{64,80},{80,64},{96,112},{112,96},{1... | collective-permute-start | bytes 786440 | tf_op jit(solution)/shard_map/ppermute | solution.py:30
  540.3 5.6 %copy-start.1 = (bf16[1,8,512,128]{3,2,1,0:T(8,128)(2,1)S(1)}, bf16[1,8,512,128]{3,2,1,0:T(8,128)(2,1)}, u32[]{:S(2)}) copy-start(bf16[1,8,512,128]{3,2,1,0:T(8,128)(2,1)} %param.22) | copy-start | bytes 3145732
Sparse Core Ops, SparseCore 0:
  10.3 56.8 all-gather.7
  69.4 38.4 all-gather.5
  110.2 37.4 all-gather.3
  239.6 296.5 reduce-scatter.1
where the time goes:
time: 562 us; the launch traced here: 552 us
  waiting for transfers between devices  340 us (60%)
  local copies, waits for them, and re-layouts  112 us (20%)
  loops' own time  31.4 us (6%)
  matrix products  26.8 us (5%)
  other arithmetic  17.6 us (3%)
  between operations  14 us (2%)
  starting transfers between devices  11.1 us (2%)
    reduce_scatter x1, waiting for transfers between devices, body(): lax.psum_scatter(terms_of_keys.astype(jnp.bfloat16), 'seq', scatter_dimen...  297 us
    all_gather x1, waiting for transfers between devices, sent_together(): lax.all_gather(both, axis, axis=dim, tiled=True)  35.5 us
    unnamed x16, local copies, waits for them, and re-layouts  29.6 us
    another operation x2, loops' own time, online_pass(): lax.scan(online_step, carried, (jnp.arange(count_of_blocks, dtype=jnp.int...  20.4 us
    dynamic_slice x24, local copies, waits for them, and re-layouts, online_pass(): lax.scan(online_step, carried, (jnp.arange(count_of_blocks, dtype=jnp.int...  14 us
    convert_element_type x1, local copies, waits for them, and re-layouts, body(): terms_of_keys.astype(jnp.bfloat16)  11.5 us
    dot_general x2, matrix products, absorb(): jnp.einsum('gjqk,kgd->qgjd', weights.astype(jnp.bfloat16), value_block, p...  11.3 us
  transfers between devices with their start and end apart: 8, of which 5 were waited for; matrix products, arithmetic and copies ran while one was open for 21% of the time, Pallas kernels for 0%

commit v1 on v0

v1 whole, which is shorter than its diff:
```python
import functools
import math

import jax
import jax.numpy as jnp
from jax import lax
from jax.experimental import pallas as pl
from jax.experimental.pallas import tpu as pltpu
from jax.sharding import PartitionSpec as P

D = 128
NS = 16
TOK = 4096
HALF = TOK // 2
ROOT = 1.0 / math.sqrt(D)
SCALE2 = ROOT * math.log2(math.e)
FLOOR = -1e30
MESH = pl.DeviceIdType.MESH
F32 = jnp.float32
BF16 = jnp.bfloat16


def dot_nt(x, y):
    return lax.dot_general(x, y, (((1,), (1,)), ((), ())), preferred_element_type=F32)


def dot_nn(x, y):
    return lax.dot_general(x, y, (((1,), (0,)), ((), ())), preferred_element_type=F32)


def wide(x, width):
    return x if width == D else jnp.concatenate([x] * (width // D), axis=1)


def absorb(query, keys, values, state, allowed=None):
    peak, acc = state
    scores = dot_nt(query, keys)
    if allowed is not None:
        scores = jnp.where(allowed, scores, FLOOR)
    top = jnp.broadcast_to(jnp.max(scores, axis=1, keepdims=True), peak.shape)
    new = jnp.maximum(peak, top)
    weights = jnp.exp2((scores - wide(new, scores.shape[1])) * SCALE2)
    fade = jnp.exp2((peak - new) * SCALE2)
    acc = acc * wide(fade, 2 * D) + dot_nn(weights.astype(BF16), values)
    return new, acc


def attend(queries, rows_at, key_ref, value_ref, full, rest_start, rest):
    rows = queries[0].shape[0]
    fresh = tuple(
        (jnp.full((rows, D), FLOOR, F32), jnp.zeros((rows, 2 * D), F32)) for _ in queries
    )

    def chunk(index, states):
        start = pl.multiple_of(index * 1024, 1024)
        keys = key_ref[pl.ds(start, 1024), :]
        values = value_ref[pl.ds(start, 1024), :]
        return tuple(absorb(q, keys, values, s) for q, s in zip(queries, states))

    states = lax.fori_loop(0, full, chunk, fresh)
    start = pl.multiple_of(rest_start, 256)
    keys = key_ref[pl.ds(start, rest), :]
    values = value_ref[pl.ds(start, rest), :]
    out = []
    for q, at, s in zip(queries, rows_at, states):
        key_pos = start + lax.broadcasted_iota(jnp.int32, (rows, rest), 1)
        row_pos = at + lax.broadcasted_iota(jnp.int32, (rows, rest), 0)
        out.append(absorb(q, keys, values, s, key_pos <= row_pos))
    return out


def student_forward(half, sq, sk, sv, ctx, lse):
    def group(sg, _):
        for sr in range(4):
            block = sg * 4 + sr
            row = pl.multiple_of(block * 128, 128)
            (peak, acc), = attend(
                [sq[pl.ds(row, 128), :]],
                [block * 256 + half * 128],
                sk, sv, sg, sg * 1024, 256 * (sr + 1),
            )
            total = acc[:, D:]
            ctx[pl.ds(row, 128), :] = acc[:, :D] / total
            log_sum = peak * SCALE2 + jnp.log2(total)
            lse[:, pl.ds(row, 128)] = jnp.transpose(log_sum)[:8, :]
        return 0

    lax.fori_loop(0, 4, group, 0)


def teacher_forward(half, heads, tq, tk, tv, tctx):
    def group(sg, _):
        for sr in range(4):
            block = sg * 4 + sr
            at = block * 256 + half * 128
            done = attend(
                [tq[block, :, h * D : (h + 1) * D] for h in heads],
                [at] * len(heads),
                tk, tv, sg, sg * 1024, 256 * (sr + 1),
            )
            for h, (_, acc) in zip(heads, done):
                tctx[block, :, h * D : (h + 1) * D] = (acc[:, :D] / acc[:, D:]).astype(BF16)
        return 0

    lax.fori_loop(0, 4, group, 0)


def mismatches(tctx, proj, ctx, grad_ctx, delta, loss):
    def step(block, _):
        row = pl.multiple_of(block * 128, 128)
        target = dot_nn(tctx[block], proj[...]).astype(BF16).astype(F32)
        context = ctx[pl.ds(row, 128), :]
        miss = context - target
        grad_ctx[pl.ds(row, 128), :] = miss.astype(BF16)
        dots = jnp.sum(miss * context, axis=1, keepdims=True)
        delta[:, pl.ds(row, 128)] = jnp.transpose(jnp.broadcast_to(dots, (128, 128)))[:8, :]
        squares = jnp.sum(miss * miss, axis=1, keepdims=True) * (1.0 / 2048.0)
        loss[block] = jnp.transpose(jnp.broadcast_to(squares, (128, 128)))[:8, :]
        return 0

    lax.fori_loop(0, NS, step, 0)


KB = 512
QB = 256


def backward(half, first, sq, sk, sv, grad_ctx, lse, delta, dqt, dkv, dq, after):
    dqt[...] = jnp.zeros(dqt.shape, F32)

    def outer(step, _):
        jb = lax.rem(first + step, TOK // KB)
        key_at = pl.multiple_of(jb * KB, KB)
        keys = sk[pl.ds(key_at, KB), :]
        values = sv[pl.ds(key_at, KB), :D]
        keys_t = jnp.transpose(keys)

        def inner(mb, carried, masked):
            dk, dv = carried
            row = pl.multiple_of(mb * QB, QB)
            query = sq[pl.ds(row, QB), :]
            grad = grad_ctx[pl.ds(row, QB), :]
            log_sum = lse[0:1, pl.ds(row, QB)]
            dots = delta[0:1, pl.ds(row, QB)]
            scores = dot_nt(keys, query)
            prob = jnp.exp2(scores * SCALE2 - log_sum)
            if masked:
                key_pos = key_at + lax.broadcasted_iota(jnp.int32, (KB, QB), 0)
                lane = lax.broadcasted_iota(jnp.int32, (KB, QB), 1)
                row_pos = mb * (2 * QB) + lane + half * 128 + jnp.where(lane >= 128, 128, 0)
                prob = jnp.where(key_pos <= row_pos, prob, 0.0)
            grad_prob = dot_nt(values, grad)
            ds = (prob * (grad_prob - dots)).astype(BF16)
            dv = dv + dot_nn(prob.astype(BF16), grad)
            dk = dk + dot_nn(ds, query)
            dqt[:, pl.ds(row, QB)] += dot_nn(keys_t, ds)
            return dk, dv

        zero = jnp.zeros((KB, D), F32)
        carried = inner(jb, (zero, zero), True)
        dk, dv = lax.fori_loop(
            jb + 1, TOK // KB, lambda mb, c: inner(mb, c, False), carried
        )
        dkv[pl.ds(key_at, KB), :D] = (dk * ROOT).astype(BF16)
        dkv[pl.ds(key_at, KB), D:] = dv.astype(BF16)
        after(jb)
        return 0

    lax.fori_loop(0, TOK // KB, outer, 0)

    def turn(block, _):
        row = pl.multiple_of(block * 128, 128)
        dq[pl.ds(row, 128), :] = jnp.transpose(dqt[:, pl.ds(row, 128)]) * ROOT
        return 0

    lax.fori_loop(0, NS, turn, 0)


class Place:
    def __init__(self):
        self.section = lax.axis_index("section")
        self.s = lax.axis_index("seq")
        self.c = lax.rem(self.section, 2)
        self.base = self.section - self.c
        self.half = lax.rem(self.s, 2)
        self.h8 = head_of(self.s)
        self.head = self.c * 8 + self.h8
        self.me = self.c * NS + self.s


def head_of(s):
    return lax.rem(lax.div(s, 2), 4) * 2 + lax.div(s, 8)


def push(here, src, dst, send, recv, c, s):
    same = jnp.logical_and(c == here.c, s == here.s)

    @pl.when(same)
    def _():
        pltpu.make_async_copy(src, dst, recv).start()

    @pl.when(jnp.logical_not(same))
    def _():
        pltpu.make_async_remote_copy(
            src_ref=src, dst_ref=dst, send_sem=send, recv_sem=recv,
            device_id={"section": here.base + c, "seq": s}, device_id_type=MESH,
        ).start()


def greet(here):
    barrier = pltpu.get_barrier_semaphore()

    def signal(t, _):
        other = lax.rem(here.me + t, 2 * NS)
        pl.semaphore_signal(
            barrier, inc=1,
            device_id={"section": here.base + lax.div(other, NS), "seq": lax.rem(other, NS)},
            device_id_type=MESH,
        )
        return 0

    lax.fori_loop(1, 2 * NS, signal, 0)
    pl.semaphore_wait(barrier, 2 * NS - 1)


def drain(ref, sem):
    pltpu.make_async_copy(ref, ref, sem).wait()


S_K, S_V, S_Q, T_K, T_V, T_Q, G_Q, G_KV, LOSS = 0, 1, 2, 3, 4, 5, 9, 10, 11
FWD = 12
N_SEM = 16


def send_student(here, sq, sk, sv, sqb, skb, svb, send, recv):
    def step(t, _):
        chip = lax.rem(here.c * 8 + lax.div(here.s, 2) + t, 16)
        c, p = lax.div(chip, 8), lax.rem(chip, 8)
        h8 = head_of(2 * p)
        kv = pl.multiple_of((2 * c + lax.div(h8, 4)) * D, D)
        q = pl.multiple_of((c * 8 + h8) * D, D)
        at = pl.multiple_of(here.s * 256 + here.c * 128, 128)
        push(here, sk.at[0, :, pl.ds(kv, D)], skb.at[pl.ds(at, 128), :],
             send.at[S_K], recv.at[S_K], c, 2 * p)
        push(here, sv.at[0, :, pl.ds(kv, D)], svb.at[pl.ds(at, 128), pl.ds(0, D)],
             send.at[S_V], recv.at[S_V], c, 2 * p + 1)
        to = pl.multiple_of(here.s * 128, 128)
        push(here, sq.at[0, :, pl.ds(q, D)], sqb.at[pl.ds(to, 128), :],
             send.at[S_Q], recv.at[S_Q], c, 2 * p + here.c)
        return 0

    lax.fori_loop(0, 16, step, 0)


def send_teacher(here, tq, tk, tv, tqb, tkb, tvb, send, recv):
    def step(t, _):
        p = lax.rem(lax.div(here.s, 2) + t, 8)
        kv = pl.multiple_of(lax.div(head_of(2 * p), 2) * D, D)
        at = pl.multiple_of(here.s * 256, 256)
        push(here, tk.at[0, :, pl.ds(kv, D)], tkb.at[pl.ds(at, 256), :],
             send.at[T_K], recv.at[T_K], here.c, 2 * p)
        push(here, tv.at[0, :, pl.ds(kv, D)], tvb.at[pl.ds(at, 256), pl.ds(0, D)],
             send.at[T_V], recv.at[T_V], here.c, 2 * p + 1)
        return 0

    lax.fori_loop(0, 8, step, 0)
    for h in range(4):
        def query(t, _):
            s = lax.rem(here.s + t, NS)
            col = pl.multiple_of(head_of(s) * 512 + h * D, D)
            row = pl.multiple_of(lax.rem(s, 2) * 128, 128)
            push(here, tq.at[0, pl.ds(row, 128), pl.ds(col, D)],
                 tqb.at[here.s, :, pl.ds(h * D, D)],
                 send.at[T_Q + h], recv.at[T_Q + h], here.c, s)
            return 0

        lax.fori_loop(0, NS, query, 0)


def sibling(here, ref, send, recv):
    return pltpu.make_async_remote_copy(
        src_ref=ref, dst_ref=ref, send_sem=send, recv_sem=recv,
        device_id={"section": here.section, "seq": here.s + 1 - 2 * here.half},
        device_id_type=MESH,
    )


def share(here, kb, vb, send, recv, k, v, fk, fv):
    values = vb.at[:, pl.ds(0, D)]

    @pl.when(here.half == 0)
    def _():
        drain(kb, recv.at[k])
        sibling(here, kb, send.at[fk], recv.at[fk]).start()
        drain(values, recv.at[fv])

    @pl.when(here.half == 1)
    def _():
        drain(values, recv.at[v])
        sibling(here, values, send.at[fv], recv.at[fv]).start()
        drain(kb, recv.at[fk])


def kernel(tq, tk, tv, proj, sq, sk, sv, out_q, out_k, out_v, out_loss,
           tqb, tkb, tvb, sqb, skb, svb, projb, ctx, lse, tctx, grad_ctx, delta, loss,
           dqt, dkv, dq, got_kv, got_loss, send, recv, local):
    here = Place()
    own_proj = pltpu.make_async_copy(proj.at[0, here.h8], projb, local)
    own_proj.start()
    greet(here)
    send_student(here, sq, sk, sv, sqb, skb, svb, send, recv)
    send_teacher(here, tq, tk, tv, tqb, tkb, tvb, send, recv)
    svb[:, D:] = jnp.ones((TOK, D), BF16)
    tvb[:, D:] = jnp.ones((TOK, D), BF16)
    share(here, skb, svb, send, recv, S_K, S_V, FWD, FWD + 1)
    drain(sqb, recv.at[S_Q])
    student_forward(here.half, sqb, skb, svb, ctx, lse)
    share(here, tkb, tvb, send, recv, T_K, T_V, FWD + 2, FWD + 3)
    for heads in ((0, 1), (2, 3)):
        for h in heads:
            drain(tqb.at[:, :, pl.ds(h * D, D)], recv.at[T_Q + h])
        teacher_forward(here.half, heads, tqb, tkb, tvb, tctx)
    own_proj.wait()
    mismatches(tctx, projb, ctx, grad_ctx, delta, loss)

    def send_loss(t, _):
        s = lax.rem(here.s + t, NS)
        push(here, loss.at[s], got_loss.at[here.head], send.at[LOSS], recv.at[LOSS], here.half, s)
        return 0

    lax.fori_loop(0, NS, send_loss, 0)
    slot = here.head * 2 + here.half

    def send_kv(jb):
        for e in range(2):
            for c in range(2):
                row = pl.multiple_of(jb * KB + e * 256 + c * 128, 128)
                push(here, dkv.at[pl.ds(row, 128), :], got_kv.at[slot],
                     send.at[G_KV], recv.at[G_KV], c, jb * 2 + e)

    backward(here.half, lax.div(here.s, 2), sqb, skb, svb, grad_ctx, lse, delta, dqt, dkv, dq,
             send_kv)

    def send_q(t, _):
        s = lax.rem(here.s + t, NS)
        row = pl.multiple_of(s * 128, 128)
        col = pl.multiple_of(here.head * D, D)
        push(here, dq.at[pl.ds(row, 128), :], out_q.at[0, :, pl.ds(col, D)],
             send.at[G_Q], recv.at[G_Q], here.half, s)
        return 0

    lax.fori_loop(0, NS, send_q, 0)

    drain(got_loss, recv.at[LOSS])
    total = got_loss[0]
    for h in range(1, 16):
        total = total + got_loss[h]
    out_loss[...] = total[0:1, :]
    drain(got_kv, recv.at[G_KV])
    for g in range(4):
        total = got_kv[g * 8].astype(F32)
        for i in range(1, 8):
            total = total + got_kv[g * 8 + i].astype(F32)
        out_k[0, :, g * D : (g + 1) * D] = total[:, :D]
        out_v[0, :, g * D : (g + 1) * D] = total[:, D:]
    drain(out_q, recv.at[G_Q])

    own_core = here.half == 0

    @pl.when(own_core)
    def _():
        drain(skb.at[pl.ds(0, 15 * 128), :], send.at[S_K])
        drain(svb.at[pl.ds(0, 16 * 128), pl.ds(0, D)], send.at[S_V])
        drain(tkb.at[pl.ds(0, 7 * 256), :], send.at[T_K])
        drain(tvb.at[pl.ds(0, 8 * 256), pl.ds(0, D)], send.at[T_V])
        drain(skb, send.at[FWD])
        drain(tkb, send.at[FWD + 2])

    @pl.when(jnp.logical_not(own_core))
    def _():
        drain(skb.at[pl.ds(0, 16 * 128), :], send.at[S_K])
        drain(svb.at[pl.ds(0, 15 * 128), pl.ds(0, D)], send.at[S_V])
        drain(tkb.at[pl.ds(0, 8 * 256), :], send.at[T_K])
        drain(tvb.at[pl.ds(0, 7 * 256), pl.ds(0, D)], send.at[T_V])
        drain(svb.at[:, pl.ds(0, D)], send.at[FWD + 1])
        drain(tvb.at[:, pl.ds(0, D)], send.at[FWD + 3])

    for h in range(4):
        drain(tqb.at[pl.ds(0, 15), :, pl.ds(h * D, D)], send.at[T_Q + h])
    drain(got_kv.at[pl.ds(0, 31)], send.at[G_KV])
    with_self = here.half == here.c

    @pl.when(with_self)
    def _():
        drain(sqb.at[pl.ds(0, 15 * 128), :], send.at[S_Q])
        drain(dq.at[pl.ds(0, 15 * 128), :], send.at[G_Q])
        drain(loss.at[pl.ds(0, 15)], send.at[LOSS])

    @pl.when(jnp.logical_not(with_self))
    def _():
        drain(sqb, send.at[S_Q])
        drain(dq, send.at[G_Q])
        drain(loss, send.at[LOSS])


def body(tq, tk, tv, proj, sq, sk, sv):
    vmem = pltpu.VMEM
    return pl.pallas_call(
        kernel,
        out_shape=(
            jax.ShapeDtypeStruct((1, 128, 2048), F32),
            jax.ShapeDtypeStruct((1, 128, 512), F32),
            jax.ShapeDtypeStruct((1, 128, 512), F32),
            jax.ShapeDtypeStruct((1, 128), F32),
        ),
        in_specs=[pl.BlockSpec(memory_space=pl.ANY)] * 7,
        out_specs=(
            pl.BlockSpec(memory_space=pl.ANY),
            pl.BlockSpec(memory_space=vmem),
            pl.BlockSpec(memory_space=vmem),
            pl.BlockSpec(memory_space=vmem),
        ),
        scratch_shapes=[
            vmem((NS, 128, 512), BF16),
            vmem((TOK, D), BF16),
            vmem((TOK, 2 * D), BF16),
            vmem((HALF, D), BF16),
            vmem((TOK, D), BF16),
            vmem((TOK, 2 * D), BF16),
            vmem((512, D), BF16),
            vmem((HALF, D), F32),
            vmem((8, HALF), F32),
            vmem((NS, 128, 512), BF16),
            vmem((HALF, D), BF16),
            vmem((8, HALF), F32),
            vmem((NS, 8, 128), F32),
            vmem((D, HALF), F32),
            vmem((TOK, 2 * D), BF16),
            vmem((HALF, D), F32),
            vmem((32, 128, 2 * D), BF16),
            vmem((16, 8, 128), F32),
            pltpu.SemaphoreType.DMA((N_SEM,)),
            pltpu.SemaphoreType.DMA((N_SEM,)),
            pltpu.SemaphoreType.DMA,
        ],
        compiler_params=pltpu.CompilerParams(
            collective_id=0, has_side_effects=True, vmem_limit_bytes=56 * 1024 * 1024
        ),
        cost_estimate=pl.CostEstimate(
            flops=17_000_000_000, bytes_accessed=8_000_000, transcendentals=30_000_000
        ),
    )(tq, tk, tv, proj, sq, sk, sv)


def solution(mesh):
    rows = P("section", "seq", None)
    return jax.shard_map(
        body,
        mesh=mesh,
        in_specs=(rows, rows, rows, P("section", None, None, None), rows, rows, rows),
        out_specs=(rows, rows, rows, P("section", "seq")),
        check_vma=False,
    )
```

time: 562 us -> 179 us (0.32); the launches traced: 552 us -> 177 us
  waiting for transfers between devices: 340 us -> 0 us
  Pallas kernels: 0 us -> 172 us
  local copies, waits for them, and re-layouts: 112 us -> 4.28 us
  loops' own time: 31.4 us -> 0 us
  matrix products: 26.8 us -> 0 us
  other arithmetic: 17.6 us -> 0 us
  between operations: 14 us -> 0.67 us
  starting transfers between devices: 11.1 us -> 0 us
    reduce_scatter x1 -> x0, waiting for transfers between devices: 297 us -> none  [body(): lax.psum_scatter(terms_of_keys.astype(jnp.bfloat16), 'seq', scatter_dimen...]
    pallas_call x0 -> x1, Pallas kernels: none -> 172 us  [body(): pl.pallas_call(kernel, out_shape=(jax.ShapeDtypeStruct((1, 128, 2048), F3...]
    all_gather x3 -> x0, waiting for transfers between devices: 35.6 us -> none  [the longest x1 35.5 us: sent_together(): lax.all_gather(both, axis, axis=dim, tiled=True)]
    another operation x27 -> x0, loops' own time: 31.4 us -> none  [the longest x2 20.4 us: online_pass(): lax.scan(online_step, carried, (jnp.arange(count_of_blocks, dtype=jnp.int...]
    reshape x4 -> x0, local copies, waits for them, and re-layouts: 27.8 us -> none  [the longest x1 7.05 us: online_pass(): value_rows.reshape(count_of_blocks, rows_per_block, heads_of_keys, head_w...]
    dot_general x10 -> x0, matrix products: 26.8 us -> none  [the longest x2 11.3 us: absorb(): jnp.einsum('gjqk,kgd->qgjd', weights.astype(jnp.bfloat16), value_block, p...]
    unnamed x16 -> x10, local copies, waits for them, and re-layouts: 29.6 us -> 4.28 us
    dynamic_slice x25 -> x0, local copies, waits for them, and re-layouts: 14.8 us -> none  [the longest x24 14 us: online_pass(): lax.scan(online_step, carried, (jnp.arange(count_of_blocks, dtype=jnp.int...]
  transfers between devices with their start and end apart: 8 -> 0, of which waited for: 5 -> 0; matrix products, arithmetic and copies ran while one was open for 21% -> 0% of each run, Pallas kernels for 0% -> 0%
where the time goes in v1:
time: 179 us; the launch traced here: 177 us
  Pallas kernels  172 us (96%)
  local copies, waits for them, and re-layouts  4.28 us (2%)
    pallas_call x1, Pallas kernels, body(): pl.pallas_call(kernel, out_shape=(jax.ShapeDtypeStruct((1, 128, 2048), F3...  172 us
    unnamed x10, local copies, waits for them, and re-layouts  4.28 us

profile of v1, /device:TPU:1, one launch (start us, length us, event | category | flops | bytes accessed | tf_op | source)
XLA Modules:
  0.0 177.0 jit_solution(15415754879379918546)
XLA Ops:
  0.6 172.0 %shard_map.102 = (f32[1,128,2048]{2,1,0:T(8,128)}, f32[1,128,512]{2,1,0:T(8,128)}, f32[1,128,512]{2,1,0:T(8,128)}, f32[1,128]{1,0:T(1,128)}) custom-call(bf16[1,256,4096]{2,1,0:T(8,128)(2,1)} %tq.1, bf16[1,256,512]{2,1,0:T(8,128)(2,1)} %tk.1, bf16[1,256,512]{2,1,0:T(8,128)(2,1)} %tv.1, bf16[1,8,512,128]{3,2,1,0:T(8,128)(2,1)} %proj.1, ...), custom_call_target="tpu_custom_call" | custom-call | flops 16999999488 | bytes 8000000 | tf_op jit(solution)/shard_map/pallas_call | solution.py:408
  172.7 0.0 copy-start.1
  172.7 0.0 copy-start
  172.7 0.0 copy-start.2
  172.7 2.3 %copy.15 = f32[1,128,2048]{2,1,0:T(8,128)} copy(f32[1,128,2048]{2,1,0:T(8,128)} %get-tuple-element.8) | data formatting | bytes 2097152
  175.1 0.0 copy-done.1
  175.1 0.7 copy.16
  175.8 0.0 copy-done
  175.8 0.7 copy.17
  176.5 0.0 copy-done.2
  176.5 0.5 copy.18
Async XLA Ops:
  172.7 2.4 %copy-start.1 = (f32[1,128,512]{2,1,0:T(8,128)S(1)}, f32[1,128,512]{2,1,0:T(8,128)}, u32[]{:S(2)}) copy-start(f32[1,128,512]{2,1,0:T(8,128)} %get-tuple-element.9) | copy-start | bytes 786436
  172.7 3.1 %copy-start = (f32[1,128,512]{2,1,0:T(8,128)S(1)}, f32[1,128,512]{2,1,0:T(8,128)}, u32[]{:S(2)}) copy-start(f32[1,128,512]{2,1,0:T(8,128)} %get-tuple-element.10) | copy-start | bytes 786436
  172.7 3.8 %copy-start.2 = (f32[1,128]{1,0:T(1,128)S(1)}, f32[1,128]{1,0:T(1,128)}, u32[]{:S(2)}) copy-start(f32[1,128]{1,0:T(1,128)} %get-tuple-element.11) | copy-start | bytes 1540

commit v2 on v1

v2 whole, which is shorter than its diff:
```python
import functools
import math

import jax
import jax.numpy as jnp
from jax import lax
from jax.experimental import pallas as pl
from jax.experimental.pallas import tpu as pltpu
from jax.sharding import PartitionSpec as P

D = 128
NS = 16
TOK = 4096
HALF = TOK // 2
ROOT = 1.0 / math.sqrt(D)
SCALE2 = ROOT * math.log2(math.e)
FLOOR = -1e30
MESH = pl.DeviceIdType.MESH
F32 = jnp.float32
BF16 = jnp.bfloat16


def dot_nt(x, y):
    return lax.dot_general(x, y, (((1,), (1,)), ((), ())), preferred_element_type=F32)


def dot_nn(x, y):
    return lax.dot_general(x, y, (((1,), (0,)), ((), ())), preferred_element_type=F32)


KC = 1024
QB = 512


def fold(x, op):
    out = x[:8]
    for i in range(8, x.shape[0], 8):
        out = op(out, x[i : i + 8])
    return out


def position(group, half):
    lane = lax.broadcasted_iota(jnp.int32, (1, QB), 1)
    return group * (2 * QB) + half * 128 + lax.div(lane, 128) * 256 + lax.rem(lane, 128)


class Flash:
    def __init__(self, half, keys, values_t, query, group, finish, score, top, total, acc):
        self.half, self.keys, self.values_t = half, keys, values_t
        self.query, self.group, self.finish = query, group, finish
        self.score, self.top, self.total, self.acc = score, top, total, acc

    def take(self, query, chunk, buf):
        span = pl.ds(pl.multiple_of(chunk * KC, KC), KC)
        scores = dot_nt(self.keys[span, :], query)
        buf[span, :] = scores
        self.top[...] = jnp.maximum(self.top[...], fold(scores, jnp.maximum))

    def take_last(self, query, chunk, buf):
        at = position(chunk, self.half)
        start = pl.multiple_of(chunk * KC, KC)
        low, high = pl.ds(start, 512), pl.ds(pl.multiple_of(start + 512, 512), 512)
        key_pos = start + lax.broadcasted_iota(jnp.int32, (512, 256), 0)
        scores = dot_nt(self.keys[low, :], query)
        near = jnp.where(key_pos <= at[:, :256], scores[:, :256], FLOOR)
        buf[low, :256] = near
        buf[low, 256:] = scores[:, 256:]
        far = dot_nt(self.keys[high, :], query[256:, :])
        far = jnp.where(key_pos + 512 <= at[:, 256:], far, FLOOR)
        buf[high, 256:] = far
        self.top[:, :256] = jnp.maximum(self.top[:, :256], fold(near, jnp.maximum))
        self.top[:, 256:] = jnp.maximum(
            self.top[:, 256:],
            jnp.maximum(fold(scores[:, 256:], jnp.maximum), fold(far, jnp.maximum)),
        )

    def mix(self, peak, chunk, buf):
        span = pl.ds(pl.multiple_of(chunk * KC, KC), KC)
        weights = jnp.exp2((buf[span, :] - peak) * SCALE2)
        self.total[...] += fold(weights, jnp.add)
        self.acc[...] += dot_nn(self.values_t[chunk], weights.astype(BF16))

    def mix_last(self, peak, chunk, buf):
        start = pl.multiple_of(chunk * KC, KC)
        low, high = pl.ds(start, 512), pl.ds(pl.multiple_of(start + 512, 512), 512)
        near = jnp.exp2((buf[low, :] - peak) * SCALE2)
        far = jnp.exp2((buf[high, 256:] - peak[:, 256:]) * SCALE2)
        self.total[...] += fold(near, jnp.add)
        self.total[:, 256:] += fold(far, jnp.add)
        self.acc[...] += dot_nn(self.values_t[chunk, :, :512], near.astype(BF16))
        self.acc[:, 256:] += dot_nn(self.values_t[chunk, :, 512:], far.astype(BF16))

    def turn(self):
        peak = jnp.max(self.top[...], axis=0, keepdims=True)
        self.top[...] = jnp.full((8, QB), FLOOR, F32)
        self.total[...] = jnp.zeros((8, QB), F32)
        self.acc[...] = jnp.zeros((D, QB), F32)
        return peak

    def end(self, task, peak):
        self.finish(task, peak, jnp.sum(self.total[...], axis=0, keepdims=True), self.acc[...])

    def lead(self, task, buf):
        self.top[...] = jnp.full((8, QB), FLOOR, F32)
        query, last = self.query(task), self.group(task)

        def one(chunk, _):
            self.take(query, chunk, buf)
            return 0

        lax.fori_loop(0, last, one, 0)
        self.take_last(query, last, buf)

    def step(self, task, old, new):
        peak = self.turn()
        done, query, last = self.group(task), self.query(task + 1), self.group(task + 1)

        def both(chunk, _):
            self.take(query, chunk, new)
            self.mix(peak, chunk, old)
            return 0

        lax.fori_loop(0, jnp.minimum(last, done), both, 0)

        @pl.when(done > last)
        def _():
            self.take_last(query, last, new)
            self.mix(peak, last, old)
            self.mix_last(peak, done, old)

        @pl.when(done < last)
        def _():
            self.mix_last(peak, done, old)
            self.take(query, done, new)
            self.take_last(query, last, new)

        @pl.when(done == last)
        def _():
            self.take_last(query, last, new)
            self.mix_last(peak, done, old)

        self.end(task, peak)

    def tail(self, task, old):
        peak = self.turn()
        done = self.group(task)

        def rest(chunk, _):
            self.mix(peak, chunk, old)
            return 0

        lax.fori_loop(0, done, rest, 0)
        self.mix_last(peak, done, old)
        self.end(task, peak)

    def run(self, tasks, ready=None):
        if ready is not None:
            ready(0)
        self.lead(0, self.score[0])

        def pair(i, _):
            self.step(2 * i, self.score[0], self.score[1])
            if ready is not None:
                ready(2 * i + 2)
            self.step(2 * i + 1, self.score[1], self.score[0])
            return 0

        lax.fori_loop(0, tasks // 2 - 1, pair, 0)
        self.step(tasks - 2, self.score[0], self.score[1])
        self.tail(tasks - 1, self.score[1])


def columns(group):
    return pl.ds(pl.multiple_of(group * QB, QB), QB)


def student_forward(half, sq, sk, svt, ctx_t, lse, work):
    def finish(task, peak, total, acc):
        at = columns(3 - task)
        ctx_t[:, at] = acc / total
        lse[:, at] = jnp.broadcast_to(peak * SCALE2 + jnp.log2(total), (8, QB))

    Flash(half, sk, svt, lambda t: sq[columns(3 - t), :], lambda t: 3 - t, finish, *work).run(4)


def teacher_forward(half, tq, tk, tvt, tctx_t, work, ready=None):
    def group(task):
        down = 3 - lax.rem(task, 4)
        return jnp.where(lax.rem(lax.div(task, 4), 2) == 0, down, 3 - down)

    def finish(task, peak, total, acc):
        row = pl.multiple_of(lax.div(task, 4) * D, D)
        tctx_t[pl.ds(row, D), columns(group(task))] = (acc / total).astype(BF16)

    Flash(half, tk, tvt, lambda t: tq[lax.div(t, 4), columns(group(t)), :], group, finish,
          *work).run(16, ready)


def turn_values(values, values_t):
    def chunk(i, _):
        values_t[i] = jnp.transpose(values[pl.ds(pl.multiple_of(i * KC, KC), KC), :])
        return 0

    lax.fori_loop(0, TOK // KC, chunk, 0)


def mismatches(tctx_t, proj, ctx_t, grad_t, delta, loss):
    proj_t = jnp.transpose(proj[...])

    def step(group, _):
        at = columns(group)
        target = dot_nn(proj_t, tctx_t[:, at]).astype(BF16).astype(F32)
        context = ctx_t[:, at]
        miss = context - target
        grad_t[:, at] = miss.astype(BF16)
        dots = jnp.sum(fold(miss * context, jnp.add), axis=0, keepdims=True)
        delta[:, at] = jnp.broadcast_to(dots, (8, QB))
        squares = jnp.sum(fold(miss * miss, jnp.add), axis=0, keepdims=True) * (1.0 / 2048.0)
        wide = jnp.broadcast_to(squares, (8, QB))
        for i in range(4):
            loss[group * 4 + i] = wide[:, i * 128 : (i + 1) * 128]
        return 0

    lax.fori_loop(0, HALF // QB, step, 0)


def backward(half, first, sq, sk, sv, grad_t, lse, delta, q_t, dq_t, dk, dv, dkv, dq, after):
    dq_t[...] = jnp.zeros(dq_t.shape, F32)
    q_t[...] = jnp.transpose(sq[...])

    def outer(step, _):
        jb = lax.rem(first + step, TOK // KC)
        start = pl.multiple_of(jb * KC, KC)
        spans = [pl.ds(pl.multiple_of(start + e * 512, 512), 512) for e in range(2)]
        turned = [jnp.transpose(sk[span, :]) for span in spans]
        dk[...] = jnp.zeros(dk.shape, F32)
        dv[...] = jnp.zeros(dv.shape, F32)

        def terms(e, at, mask=None):
            query_t, grad = q_t[:, at], grad_t[:, at]
            prob = jnp.exp2(dot_nn(sk[spans[e], :], query_t) * SCALE2 - lse[0:1, at])
            if mask is not None:
                prob = jnp.where(mask, prob, 0.0)
            ds = (prob * (dot_nn(sv[spans[e], :], grad) - delta[0:1, at])).astype(BF16)
            keys = slice(e * 512, (e + 1) * 512)
            dv[:, keys] += dot_nt(grad, prob.astype(BF16))
            dk[:, keys] += dot_nt(query_t, ds)
            dq_t[:, at] += dot_nn(turned[e], ds)

        key_pos = start + lax.broadcasted_iota(jnp.int32, (512, QB), 0)
        at = position(jb, half)
        terms(0, columns(jb), key_pos <= at)
        late = pl.ds(pl.multiple_of(jb * QB + 256, 256), 256)
        terms(1, late, key_pos[:, 256:] + 512 <= at[:, 256:])

        def full(group, _):
            terms(0, columns(group))
            terms(1, columns(group))
            return 0

        lax.fori_loop(jb + 1, HALF // QB, full, 0)
        for i in range(KC // 128):
            span = slice(i * 128, (i + 1) * 128)
            dkv[jb * 4 + i // 2, i % 2, :D, :] = (dk[:, span] * ROOT).astype(BF16)
            dkv[jb * 4 + i // 2, i % 2, D:, :] = dv[:, span].astype(BF16)
        after(step, jb)
        return 0

    lax.fori_loop(0, TOK // KC, outer, 0)

    def turn(group, _):
        dq[columns(group), :] = (jnp.transpose(dq_t[:, columns(group)]) * ROOT).astype(BF16)
        return 0

    lax.fori_loop(0, HALF // QB, turn, 0)


class Place:
    def __init__(self):
        self.section = lax.axis_index("section")
        self.s = lax.axis_index("seq")
        self.c = lax.rem(self.section, 2)
        self.base = self.section - self.c
        self.half = lax.rem(self.s, 2)
        self.h8 = head_of(self.s)
        self.head = self.c * 8 + self.h8
        self.me = self.c * NS + self.s


def head_of(s):
    return lax.rem(lax.div(s, 2), 4) * 2 + lax.div(s, 8)


def push(here, src, dst, send, recv, c, s):
    same = jnp.logical_and(c == here.c, s == here.s)

    @pl.when(same)
    def _():
        pltpu.make_async_copy(src, dst, recv).start()

    @pl.when(jnp.logical_not(same))
    def _():
        pltpu.make_async_remote_copy(
            src_ref=src, dst_ref=dst, send_sem=send, recv_sem=recv,
            device_id={"section": here.base + c, "seq": s}, device_id_type=MESH,
        ).start()


def greet(here):
    barrier = pltpu.get_barrier_semaphore()

    def signal(t, _):
        other = lax.rem(here.me + t, 2 * NS)
        pl.semaphore_signal(
            barrier, inc=1,
            device_id={"section": here.base + lax.div(other, NS), "seq": lax.rem(other, NS)},
            device_id_type=MESH,
        )
        return 0

    lax.fori_loop(1, 2 * NS, signal, 0)
    pl.semaphore_wait(barrier, 2 * NS - 1)


def drain(ref, sem):
    pltpu.make_async_copy(ref, ref, sem).wait()


S_K, S_V, S_Q, T_K, T_V, T_Q, G_Q, G_KV, LOSS = 0, 1, 2, 3, 4, 5, 9, 10, 11
FWD = 12
PAIR = 16
N_SEM = 20


def send_student(here, sq, sk, sv, sqb, skb, svb, send, recv):
    def step(t, _):
        chip = lax.rem(here.c * 8 + lax.div(here.s, 2) + t, 16)
        c, p = lax.div(chip, 8), lax.rem(chip, 8)
        h8 = head_of(2 * p)
        kv = pl.multiple_of((2 * c + lax.div(h8, 4)) * D, D)
        q = pl.multiple_of((c * 8 + h8) * D, D)
        at = pl.multiple_of(here.s * 256 + here.c * 128, 128)
        push(here, sk.at[0, :, pl.ds(kv, D)], skb.at[pl.ds(at, 128), :],
             send.at[S_K], recv.at[S_K], c, 2 * p)
        push(here, sv.at[0, :, pl.ds(kv, D)], svb.at[pl.ds(at, 128), :],
             send.at[S_V], recv.at[S_V], c, 2 * p + 1)
        to = pl.multiple_of(here.s * 128, 128)
        push(here, sq.at[0, :, pl.ds(q, D)], sqb.at[pl.ds(to, 128), :],
             send.at[S_Q], recv.at[S_Q], c, 2 * p + here.c)
        return 0

    lax.fori_loop(0, 16, step, 0)


def send_teacher(here, tq, tk, tv, tqb, tkb, tvb, send, recv):
    def step(t, _):
        p = lax.rem(lax.div(here.s, 2) + t, 8)
        kv = pl.multiple_of(lax.div(head_of(2 * p), 2) * D, D)
        at = pl.multiple_of(here.s * 256, 256)
        push(here, tk.at[0, :, pl.ds(kv, D)], tkb.at[pl.ds(at, 256), :],
             send.at[T_K], recv.at[T_K], here.c, 2 * p)
        push(here, tv.at[0, :, pl.ds(kv, D)], tvb.at[pl.ds(at, 256), :],
             send.at[T_V], recv.at[T_V], here.c, 2 * p + 1)
        return 0

    lax.fori_loop(0, 8, step, 0)
    for h in range(4):
        def query(t, _):
            s = lax.rem(here.s + t, NS)
            col = pl.multiple_of(head_of(s) * 512 + h * D, D)
            row = pl.multiple_of(lax.rem(s, 2) * 128, 128)
            push(here, tq.at[0, pl.ds(row, 128), pl.ds(col, D)],
                 tqb.at[h, pl.ds(pl.multiple_of(here.s * 128, 128), 128), :],
                 send.at[T_Q + h], recv.at[T_Q + h], here.c, s)
            return 0

        lax.fori_loop(0, NS, query, 0)


def sibling(here, src, dst, send, recv):
    return pltpu.make_async_remote_copy(
        src_ref=src, dst_ref=dst, send_sem=send, recv_sem=recv,
        device_id={"section": here.section, "seq": here.s + 1 - 2 * here.half},
        device_id_type=MESH,
    )


def share(here, kb, vb, send, recv, k, v, fk, fv):
    @pl.when(here.half == 0)
    def _():
        drain(kb, recv.at[k])
        sibling(here, kb, kb, send.at[fk], recv.at[fk]).start()
        drain(vb, recv.at[fv])

    @pl.when(here.half == 1)
    def _():
        drain(vb, recv.at[v])
        sibling(here, vb, vb, send.at[fv], recv.at[fv]).start()
        drain(kb, recv.at[fk])


def kernel(tq, tk, tv, proj, sq, sk, sv, out_q, out_k, out_v, out_loss,
           tqb, tkb, tvb, tvt, sqb, skb, svb, svt, projb, ctx_t, lse, tctx_t, grad_t, delta, loss,
           q_t, dq_t, dk, dv, dkv, paired, summed, dq, got_kv, got_loss,
           score0, score1, top, total, acc, send, recv, local):
    here = Place()
    work = ((score0, score1), top, total, acc)
    own_proj = pltpu.make_async_copy(proj.at[0, here.h8], projb, local)
    own_proj.start()
    greet(here)
    send_student(here, sq, sk, sv, sqb, skb, svb, send, recv)
    send_teacher(here, tq, tk, tv, tqb, tkb, tvb, send, recv)
    share(here, skb, svb, send, recv, S_K, S_V, FWD, FWD + 1)
    turn_values(svb, svt)
    drain(sqb, recv.at[S_Q])
    student_forward(here.half, sqb, skb, svt, ctx_t, lse, work)
    share(here, tkb, tvb, send, recv, T_K, T_V, FWD + 2, FWD + 3)
    turn_values(tvb, tvt)

    def ready(task):
        head = lax.div(task, 4)

        @pl.when(lax.rem(task, 4) == 0)
        def _():
            drain(tqb.at[head], recv.at[T_Q + head])

    teacher_forward(here.half, tqb, tkb, tvt, tctx_t, work, ready)
    own_proj.wait()
    mismatches(tctx_t, projb, ctx_t, grad_t, delta, loss)

    def send_loss(t, _):
        s = lax.rem(here.s + t, NS)
        push(here, loss.at[s], got_loss.at[here.head], send.at[LOSS], recv.at[LOSS], here.half, s)
        return 0

    lax.fori_loop(0, NS, send_loss, 0)
    first = lax.rem(lax.div(here.s, 2), 4)

    def finish_kv(step):
        jb = lax.rem(first + step, 4)
        drain(paired.at[step], recv.at[PAIR + step])

        def one(i, _):
            s = jb * 4 + i
            mine = dkv[s, here.half].astype(F32) + paired[step, i].astype(F32)
            summed[s] = mine.astype(BF16)
            push(here, summed.at[s], got_kv.at[here.head], send.at[G_KV], recv.at[G_KV],
                 here.half, s)
            return 0

        lax.fori_loop(0, 4, one, 0)

    def after(step, jb):
        sibling(here, dkv.at[pl.ds(jb * 4, 4), 1 - here.half], paired.at[step],
                send.at[PAIR], recv.at[PAIR + step]).start()

        @pl.when(step > 0)
        def _():
            finish_kv(step - 1)

    backward(here.half, first, sqb, skb, svb, grad_t, lse, delta, q_t, dq_t, dk, dv, dkv, dq, after)

    def send_q(t, _):
        s = lax.rem(here.s + t, NS)
        row = pl.multiple_of(s * 128, 128)
        col = pl.multiple_of(here.head * D, D)
        push(here, dq.at[pl.ds(row, 128), :], out_q.at[0, :, pl.ds(col, D)],
             send.at[G_Q], recv.at[G_Q], here.half, s)
        return 0

    finish_kv(3)
    lax.fori_loop(0, NS, send_q, 0)

    drain(got_loss, recv.at[LOSS])
    sums = got_loss[0]
    for h in range(1, 16):
        sums = sums + got_loss[h]
    out_loss[...] = sums[0:1, :]
    drain(got_kv, recv.at[G_KV])
    for g in range(4):
        sums = got_kv[g * 4].astype(F32)
        for i in range(1, 4):
            sums = sums + got_kv[g * 4 + i].astype(F32)
        out_k[0, :, g * D : (g + 1) * D] = jnp.transpose(sums[:D])
        out_v[0, :, g * D : (g + 1) * D] = jnp.transpose(sums[D:])
    drain(out_q, recv.at[G_Q])

    own_core = here.half == 0

    @pl.when(own_core)
    def _():
        drain(skb.at[pl.ds(0, 15 * 128), :], send.at[S_K])
        drain(svb.at[pl.ds(0, 16 * 128), :], send.at[S_V])
        drain(tkb.at[pl.ds(0, 7 * 256), :], send.at[T_K])
        drain(tvb.at[pl.ds(0, 8 * 256), :], send.at[T_V])
        drain(skb, send.at[FWD])
        drain(tkb, send.at[FWD + 2])

    @pl.when(jnp.logical_not(own_core))
    def _():
        drain(skb.at[pl.ds(0, 16 * 128), :], send.at[S_K])
        drain(svb.at[pl.ds(0, 15 * 128), :], send.at[S_V])
        drain(tkb.at[pl.ds(0, 8 * 256), :], send.at[T_K])
        drain(tvb.at[pl.ds(0, 7 * 256), :], send.at[T_V])
        drain(svb, send.at[FWD + 1])
        drain(tvb, send.at[FWD + 3])

    for h in range(4):
        drain(tqb.at[h, pl.ds(0, 15 * 128), :], send.at[T_Q + h])
    drain(paired, send.at[PAIR])
    with_self = here.half == here.c

    @pl.when(with_self)
    def _():
        drain(sqb.at[pl.ds(0, 15 * 128), :], send.at[S_Q])
        drain(dq.at[pl.ds(0, 15 * 128), :], send.at[G_Q])
        drain(loss.at[pl.ds(0, 15)], send.at[LOSS])
        drain(got_kv.at[pl.ds(0, 15)], send.at[G_KV])

    @pl.when(jnp.logical_not(with_self))
    def _():
        drain(sqb, send.at[S_Q])
        drain(dq, send.at[G_Q])
        drain(loss, send.at[LOSS])
        drain(got_kv, send.at[G_KV])


def body(tq, tk, tv, proj, sq, sk, sv):
    vmem = pltpu.VMEM
    dq, dk, dv, loss = pl.pallas_call(
        kernel,
        out_shape=(
            jax.ShapeDtypeStruct((1, 128, 2048), BF16),
            jax.ShapeDtypeStruct((1, 128, 512), F32),
            jax.ShapeDtypeStruct((1, 128, 512), F32),
            jax.ShapeDtypeStruct((1, 128), F32),
        ),
        in_specs=[pl.BlockSpec(memory_space=pl.ANY)] * 7,
        out_specs=(
            pl.BlockSpec(memory_space=pl.ANY),
            pl.BlockSpec(memory_space=vmem),
            pl.BlockSpec(memory_space=vmem),
            pl.BlockSpec(memory_space=vmem),
        ),
        scratch_shapes=[
            vmem((4, HALF, D), BF16),
            vmem((TOK, D), BF16),
            vmem((TOK, D), BF16),
            vmem((TOK // KC, D, KC), BF16),
            vmem((HALF, D), BF16),
            vmem((TOK, D), BF16),
            vmem((TOK, D), BF16),
            vmem((TOK // KC, D, KC), BF16),
            vmem((512, D), BF16),
            vmem((D, HALF), F32),
            vmem((8, HALF), F32),
            vmem((4 * D, HALF), BF16),
            vmem((D, HALF), BF16),
            vmem((8, HALF), F32),
            vmem((NS, 8, 128), F32),
            vmem((D, HALF), BF16),
            vmem((D, HALF), F32),
            vmem((D, KC), F32),
            vmem((D, KC), F32),
            vmem((NS, 2, 2 * D, 128), BF16),
            vmem((4, 4, 2 * D, 128), BF16),
            vmem((NS, 2 * D, 128), BF16),
            vmem((HALF, D), BF16),
            vmem((NS, 2 * D, 128), BF16),
            vmem((NS, 8, 128), F32),
            vmem((TOK, QB), F32),
            vmem((TOK, QB), F32),
            vmem((8, QB), F32),
            vmem((8, QB), F32),
            vmem((D, QB), F32),
            pltpu.SemaphoreType.DMA((N_SEM,)),
            pltpu.SemaphoreType.DMA((N_SEM,)),
            pltpu.SemaphoreType.DMA,
        ],
        compiler_params=pltpu.CompilerParams(
            collective_id=0, has_side_effects=True, vmem_limit_bytes=56 * 1024 * 1024
        ),
        cost_estimate=pl.CostEstimate(
            flops=17_000_000_000, bytes_accessed=8_000_000, transcendentals=30_000_000
        ),
    )(tq, tk, tv, proj, sq, sk, sv)
    return dq.astype(F32), dk, dv, loss


def solution(mesh):
    rows = P("section", "seq", None)
    return jax.shard_map(
        body,
        mesh=mesh,
        in_specs=(rows, rows, rows, P("section", None, None, None), rows, rows, rows),
        out_specs=(rows, rows, rows, P("section", "seq")),
        check_vma=False,
    )
```

time: 179 us -> 126 us (0.70); the launches traced: 177 us -> 126 us
  Pallas kernels: 172 us -> 121 us
  other arithmetic: 0 us -> 2.16 us
    pallas_call x1, Pallas kernels: 172 us -> 121 us  [body(): pl.pallas_call(kernel, out_shape=(jax.ShapeDtypeStruct((1, 128, 2048), BF...]
    convert_element_type x0 -> x1, other arithmetic: none -> 2.16 us  [body(): return (dq.astype(F32), dk, dv, loss)]
    unnamed x10 -> x7, local copies, waits for them, and re-layouts: 4.28 us -> 2.89 us
where the time goes in v2:
time: 126 us
  Pallas kernels  121 us (96%)
  local copies, waits for them, and re-layouts  2.89 us (2%)
  other arithmetic  2.16 us (2%)
    pallas_call x1, Pallas kernels, body(): pl.pallas_call(kernel, out_shape=(jax.ShapeDtypeStruct((1, 128, 2048), BF...  121 us
    unnamed x7, local copies, waits for them, and re-layouts  2.89 us

profile of v2, /device:TPU:1, one launch (start us, length us, event | category | flops | bytes accessed | tf_op | source)
XLA Modules:
  0.0 126.2 jit_solution(9368715122963228648)
XLA Ops:
  0.6 120.5 %shard_map.102 = (bf16[1,128,2048]{2,1,0:T(8,128)(2,1)}, f32[1,128,512]{2,1,0:T(8,128)}, f32[1,128,512]{2,1,0:T(8,128)}, f32[1,128]{1,0:T(1,128)}) custom-call(bf16[1,256,4096]{2,1,0:T(8,128)(2,1)} %tq.1, bf16[1,256,512]{2,1,0:T(8,128)(2,1)} %tk.1, bf16[1,256,512]{2,1,0:T(8,128)(2,1)} %tv.1, bf16[1,8,512,128]{3,2,1,0:T(8,128)(2,1)} %proj.1, ...), custom_call_target="tpu_custom_call" | custom-call | flops 16999999488 | bytes 8000000 | tf_op jit(solution)/shard_map/pallas_call | solution.py:530
  121.2 0.0 copy-start
  121.2 0.0 copy-start.1
  121.2 2.2 %convert_element_type.3 = f32[1,128,2048]{2,1,0:T(8,128)} convert(bf16[1,128,2048]{2,1,0:T(8,128)(2,1)} %get-tuple-element.8) | non-fusion elementwise | flops 262144 | bytes 1572864 | tf_op jit(solution)/shard_map/convert_element_type | solution.py:587
  123.4 1.7 %copy.14 = f32[1,128,512]{2,1,0:T(8,128)} copy(f32[1,128,512]{2,1,0:T(8,128)} %get-tuple-element.17) | data formatting | bytes 524288
  125.0 0.0 copy-done
  125.0 0.7 copy.15
  125.7 0.0 copy-done.1
  125.7 0.5 copy.16
Async XLA Ops:
  121.2 3.9 %copy-start = (f32[1,128,512]{2,1,0:T(8,128)S(1)}, f32[1,128,512]{2,1,0:T(8,128)}, u32[]{:S(2)}) copy-start(f32[1,128,512]{2,1,0:T(8,128)} %get-tuple-element.18) | copy-start | bytes 786436
  121.2 4.5 %copy-start.1 = (f32[1,128]{1,0:T(1,128)S(1)}, f32[1,128]{1,0:T(1,128)}, u32[]{:S(2)}) copy-start(f32[1,128]{1,0:T(1,128)} %get-tuple-element.19) | copy-start | bytes 1540

commit v3 on v2

--- a/solution.py
+++ b/solution.py
@@ -45,155 +45,135 @@
 
 
 class Flash:
-    def __init__(self, half, keys, values_t, query, group, finish, score, top, total, acc):
-        self.half, self.keys, self.values_t = half, keys, values_t
-        self.query, self.group, self.finish = query, group, finish
-        self.score, self.top, self.total, self.acc = score, top, total, acc
-
-    def take(self, query, chunk, buf):
-        span = pl.ds(pl.multiple_of(chunk * KC, KC), KC)
+    def __init__(self, half, keys, values_t, finish, top):
+        self.half, self.keys, self.values_t, self.finish, self.top = half, keys, values_t, finish, top
+
+    def take(self, top, query, chunk, buf):
+        span = slice(chunk * KC, (chunk + 1) * KC)
         scores = dot_nt(self.keys[span, :], query)
         buf[span, :] = scores
-        self.top[...] = jnp.maximum(self.top[...], fold(scores, jnp.maximum))
-
-    def take_last(self, query, chunk, buf):
+        return jnp.maximum(top, fold(scores, jnp.maximum))
+
+    def take_last(self, top, query, chunk, buf):
         at = position(chunk, self.half)
-        start = pl.multiple_of(chunk * KC, KC)
-        low, high = pl.ds(start, 512), pl.ds(pl.multiple_of(start + 512, 512), 512)
+        start = chunk * KC
+        low, high = slice(start, start + 512), slice(start + 512, start + 1024)
         key_pos = start + lax.broadcasted_iota(jnp.int32, (512, 256), 0)
         scores = dot_nt(self.keys[low, :], query)
+        far = dot_nt(self.keys[high, :], query[256:, :])
         near = jnp.where(key_pos <= at[:, :256], scores[:, :256], FLOOR)
+        far = jnp.where(key_pos + 512 <= at[:, 256:], far, FLOOR)
         buf[low, :256] = near
         buf[low, 256:] = scores[:, 256:]
-        far = dot_nt(self.keys[high, :], query[256:, :])
-        far = jnp.where(key_pos + 512 <= at[:, 256:], far, FLOOR)
         buf[high, 256:] = far
-        self.top[:, :256] = jnp.maximum(self.top[:, :256], fold(near, jnp.maximum))
-        self.top[:, 256:] = jnp.maximum(
-            self.top[:, 256:],
-            jnp.maximum(fold(scores[:, 256:], jnp.maximum), fold(far, jnp.maximum)),
+        right = jnp.maximum(fold(scores[:, 256:], jnp.maximum), fold(far, jnp.maximum))
+        return jnp.maximum(top, jnp.concatenate([fold(near, jnp.maximum), right], axis=1))
+
+    def mix(self, state, peak, chunk, buf):
+        total, acc = state
+        weights = jnp.exp2((buf[chunk * KC : (chunk + 1) * KC, :] - peak) * SCALE2)
+        total = total + fold(weights, jnp.add)
+        return total, acc + dot_nn(self.values_t[chunk], weights.astype(BF16))
+
+    def mix_last(self, state, peak, chunk, buf):
+        total, acc = state
+        start = chunk * KC
+        near = jnp.exp2((buf[start : start + 512, :] - peak) * SCALE2)
+        far = jnp.exp2((buf[start + 512 : start + 1024, 256:] - peak[:, 256:]) * SCALE2)
+        sums = fold(near, jnp.add)
+        total = total + jnp.concatenate(
+            [sums[:, :256], sums[:, 256:] + fold(far, jnp.add)], axis=1
         )
-
-    def mix(self, peak, chunk, buf):
-        span = pl.ds(pl.multiple_of(chunk * KC, KC), KC)
-        weights = jnp.exp2((buf[span, :] - peak) * SCALE2)
-        self.total[...] += fold(weights, jnp.add)
-        self.acc[...] += dot_nn(self.values_t[chunk], weights.astype(BF16))
-
-    def mix_last(self, peak, chunk, buf):
-        start = pl.multiple_of(chunk * KC, KC)
-        low, high = pl.ds(start, 512), pl.ds(pl.multiple_of(start + 512, 512), 512)
-        near = jnp.exp2((buf[low, :] - peak) * SCALE2)
-        far = jnp.exp2((buf[high, 256:] - peak[:, 256:]) * SCALE2)
-        self.total[...] += fold(near, jnp.add)
-        self.total[:, 256:] += fold(far, jnp.add)
-        self.acc[...] += dot_nn(self.values_t[chunk, :, :512], near.astype(BF16))
-        self.acc[:, 256:] += dot_nn(self.values_t[chunk, :, 512:], far.astype(BF16))
-
-    def turn(self):
-        peak = jnp.max(self.top[...], axis=0, keepdims=True)
-        self.top[...] = jnp.full((8, QB), FLOOR, F32)
-        self.total[...] = jnp.zeros((8, QB), F32)
-        self.acc[...] = jnp.zeros((D, QB), F32)
-        return peak
-
-    def end(self, task, peak):
-        self.finish(task, peak, jnp.sum(self.total[...], axis=0, keepdims=True), self.acc[...])
-
-    def lead(self, task, buf):
-        self.top[...] = jnp.full((8, QB), FLOOR, F32)
-        query, last = self.query(task), self.group(task)
-
-        def one(chunk, _):
-            self.take(query, chunk, buf)
-            return 0
-
-        lax.fori_loop(0, last, one, 0)
-        self.take_last(query, last, buf)
-
-    def step(self, task, old, new):
-        peak = self.turn()
-        done, query, last = self.group(task), self.query(task + 1), self.group(task + 1)
-
-        def both(chunk, _):
-            self.take(query, chunk, new)
-            self.mix(peak, chunk, old)
-            return 0
-
-        lax.fori_loop(0, jnp.minimum(last, done), both, 0)
-
-        @pl.when(done > last)
+        near = dot_nn(self.values_t[chunk, :, :512], near.astype(BF16))
+        far = dot_nn(self.values_t[chunk, :, 512:], far.astype(BF16))
+        return total, acc + jnp.concatenate([near[:, :256], near[:, 256:] + far], axis=1)
+
+    def step(self, task, old, following, new):
+        peak = top = None
+        state = (jnp.zeros((8, QB), F32), jnp.zeros((D, QB), F32))
+        mixes, takes = [], []
+        if task is not None:
+            peak = jnp.max(self.top[...], axis=0, keepdims=True)
+            mixes = list(range(task[0] + 1))
+        if following is not None:
+            query = following[1]()
+            top = jnp.full((8, QB), FLOOR, F32)
+            takes = list(range(following[0] + 1))
+        for chunk in range(max(len(mixes), len(takes))):
+            if chunk < len(takes):
+                step = self.take_last if chunk == following[0] else self.take
+                top = step(top, query, chunk, new)
+            if chunk < len(mixes):
+                step = self.mix_last if chunk == task[0] else self.mix
+                state = step(state, peak, chunk, old)
+        if following is not None:
+            self.top[...] = top
+        if task is not None:
+            task[2](peak, jnp.sum(state[0], axis=0, keepdims=True), state[1])
+
+
+def columns(group):
+    if isinstance(group, int):
+        return slice(group * QB, (group + 1) * QB)
+    return pl.ds(pl.multiple_of(group * QB, QB), QB)
+
+
+def student_forward(half, sq, sk, svt, ctx_t, lse, work):
+    score, top = work
+    flash = Flash(half, sk, svt, None, top)
+
+    def task(group):
+        at = columns(group)
+
+        def finish(peak, total, acc):
+            ctx_t[:, at] = acc / total
+            lse[:, at] = jnp.broadcast_to(peak * SCALE2 + jnp.log2(total), (8, QB))
+
+        return group, lambda: sq[at, :], finish
+
+    tasks = [task(group) for group in (3, 2, 1, 0)]
+    flash.step(None, None, tasks[0], score[0])
+    for k in range(4):
+        following = tasks[k + 1] if k < 3 else None
+        flash.step(tasks[k], score[k % 2], following, score[(k + 1) % 2])
+
+
+def teacher_forward(half, tq, tk, tvt, tctx_t, work, ready):
+    score, top = work
+    flash = Flash(half, tk, tvt, None, top)
+
+    def task(head, group):
+        at = columns(group)
+
+        def finish(peak, total, acc):
+            row = pl.multiple_of(head * D, D)
+            tctx_t[pl.ds(row, D), at] = (acc / total).astype(BF16)
+
+        return group, lambda: tq[head, at, :], finish
+
+    ready(0)
+    flash.step(None, None, task(0, 3), score[0])
+
+    def pair(i, _):
+        tasks = [task(2 * i, group) for group in (3, 2, 1, 0)]
+        tasks += [task(2 * i + 1, group) for group in (0, 1, 2, 3)]
+        for k in range(7):
+            if k == 3:
+                ready(2 * i + 1)
+            flash.step(tasks[k], score[k % 2], tasks[k + 1], score[(k + 1) % 2])
+
+        @pl.when(i == 0)
         def _():
-            self.take_last(query, last, new)
-            self.mix(peak, last, old)
-            self.mix_last(peak, done, old)
-
-        @pl.when(done < last)
+            ready(2)
+            flash.step(tasks[7], score[1], task(2, 3), score[0])
+
+        @pl.when(i == 1)
         def _():
-            self.mix_last(peak, done, old)
-            self.take(query, done, new)
-            self.take_last(query, last, new)
-
-        @pl.when(done == last)
-        def _():
-            self.take_last(query, last, new)
-            self.mix_last(peak, done, old)
-
-        self.end(task, peak)
-
-    def tail(self, task, old):
-        peak = self.turn()
-        done = self.group(task)
-
-        def rest(chunk, _):
-            self.mix(peak, chunk, old)
-            return 0
-
-        lax.fori_loop(0, done, rest, 0)
-        self.mix_last(peak, done, old)
-        self.end(task, peak)
-
-    def run(self, tasks, ready=None):
-        if ready is not None:
-            ready(0)
-        self.lead(0, self.score[0])
-
-        def pair(i, _):
-            self.step(2 * i, self.score[0], self.score[1])
-            if ready is not None:
-                ready(2 * i + 2)
-            self.step(2 * i + 1, self.score[1], self.score[0])
-            return 0
-
-        lax.fori_loop(0, tasks // 2 - 1, pair, 0)
-        self.step(tasks - 2, self.score[0], self.score[1])
-        self.tail(tasks - 1, self.score[1])
-
-
-def columns(group):
-    return pl.ds(pl.multiple_of(group * QB, QB), QB)
-
-
-def student_forward(half, sq, sk, svt, ctx_t, lse, work):
-    def finish(task, peak, total, acc):
-        at = columns(3 - task)
-        ctx_t[:, at] = acc / total
-        lse[:, at] = jnp.broadcast_to(peak * SCALE2 + jnp.log2(total), (8, QB))
-
-    Flash(half, sk, svt, lambda t: sq[columns(3 - t), :], lambda t: 3 - t, finish, *work).run(4)
-
-
-def teacher_forward(half, tq, tk, tvt, tctx_t, work, ready=None):
-    def group(task):
-        down = 3 - lax.rem(task, 4)
-        return jnp.where(lax.rem(lax.div(task, 4), 2) == 0, down, 3 - down)
-
-    def finish(task, peak, total, acc):
-        row = pl.multiple_of(lax.div(task, 4) * D, D)
-        tctx_t[pl.ds(row, D), columns(group(task))] = (acc / total).astype(BF16)
-
-    Flash(half, tk, tvt, lambda t: tq[lax.div(t, 4), columns(group(t)), :], group, finish,
-          *work).run(16, ready)
+            flash.step(tasks[7], score[1], None, None)
+
+        return 0
+
+    lax.fori_loop(0, 2, pair, 0)
 
 
 def turn_values(values, values_t):
@@ -224,7 +204,7 @@
     lax.fori_loop(0, HALF // QB, step, 0)
 
 
-def backward(half, first, sq, sk, sv, grad_t, lse, delta, q_t, dq_t, dk, dv, dkv, dq, after):
+def backward(half, first, sq, sk, sv, grad_t, lse, delta, q_t, dq_t, dk, dv, dkv, dq, middle, after, send_dq):
     dq_t[...] = jnp.zeros(dq_t.shape, F32)
     q_t[...] = jnp.transpose(sq[...])
 
@@ -253,9 +233,25 @@
         late = pl.ds(pl.multiple_of(jb * QB + 256, 256), 256)
         terms(1, late, key_pos[:, 256:] + 512 <= at[:, 256:])
 
+        def leave(group):
+            at = columns(group)
+            dq[at, :] = (jnp.transpose(dq_t[:, at]) * ROOT).astype(BF16)
+            send_dq(group)
+
+        middle(step)
+
+        @pl.when(jnp.logical_or(step + first >= TOK // KC, jnp.logical_and(first == 0, step >= 0)))
+        def _():
+            leave(jb)
+
         def full(group, _):
             terms(0, columns(group))
             terms(1, columns(group))
+
+            @pl.when(jnp.logical_and(step == TOK // KC - 1, first > 0))
+            def _():
+                leave(group)
+
             return 0
 
         lax.fori_loop(jb + 1, HALF // QB, full, 0)
@@ -267,12 +263,6 @@
         return 0
 
     lax.fori_loop(0, TOK // KC, outer, 0)
-
-    def turn(group, _):
-        dq[columns(group), :] = (jnp.transpose(dq_t[:, columns(group)]) * ROOT).astype(BF16)
-        return 0
-
-    lax.fori_loop(0, HALF // QB, turn, 0)
 
 
 class Place:
@@ -334,7 +324,7 @@
 
 def send_student(here, sq, sk, sv, sqb, skb, svb, send, recv):
     def step(t, _):
-        chip = lax.rem(here.c * 8 + lax.div(here.s, 2) + t, 16)
+        chip = lax.rem(here.c * 8 + lax.div(here.s, 2) + jnp.where(here.half == 0, t, 16 - t), 16)
         c, p = lax.div(chip, 8), lax.rem(chip, 8)
         h8 = head_of(2 * p)
         kv = pl.multiple_of((2 * c + lax.div(h8, 4)) * D, D)
@@ -354,7 +344,7 @@
 
 def send_teacher(here, tq, tk, tv, tqb, tkb, tvb, send, recv):
     def step(t, _):
-        p = lax.rem(lax.div(here.s, 2) + t, 8)
+        p = lax.rem(lax.div(here.s, 2) + jnp.where(here.half == 0, t, 8 - t), 8)
         kv = pl.multiple_of(lax.div(head_of(2 * p), 2) * D, D)
         at = pl.multiple_of(here.s * 256, 256)
         push(here, tk.at[0, :, pl.ds(kv, D)], tkb.at[pl.ds(at, 256), :],
@@ -366,15 +356,15 @@
     lax.fori_loop(0, 8, step, 0)
     for h in range(4):
         def query(t, _):
-            s = lax.rem(here.s + t, NS)
-            col = pl.multiple_of(head_of(s) * 512 + h * D, D)
-            row = pl.multiple_of(lax.rem(s, 2) * 128, 128)
-            push(here, tq.at[0, pl.ds(row, 128), pl.ds(col, D)],
-                 tqb.at[h, pl.ds(pl.multiple_of(here.s * 128, 128), 128), :],
-                 send.at[T_Q + h], recv.at[T_Q + h], here.c, s)
+            p = lax.rem(lax.div(here.s, 2) + jnp.where(here.half == 0, t, 8 - t), 8)
+            col = pl.multiple_of(head_of(2 * p) * 512 + h * D, D)
+            for core in range(2):
+                push(here, tq.at[0, pl.ds(core * 128, 128), pl.ds(col, D)],
+                     tqb.at[h, pl.ds(pl.multiple_of(here.s * 128, 128), 128), :],
+                     send.at[T_Q + h], recv.at[T_Q + h], here.c, 2 * p + core)
             return 0
 
-        lax.fori_loop(0, NS, query, 0)
+        lax.fori_loop(0, 8, query, 0)
 
 
 def sibling(here, src, dst, send, recv):
@@ -402,9 +392,9 @@
 def kernel(tq, tk, tv, proj, sq, sk, sv, out_q, out_k, out_v, out_loss,
            tqb, tkb, tvb, tvt, sqb, skb, svb, svt, projb, ctx_t, lse, tctx_t, grad_t, delta, loss,
            q_t, dq_t, dk, dv, dkv, paired, summed, dq, got_kv, got_loss,
-           score0, score1, top, total, acc, send, recv, local):
+           score0, score1, top, send, recv, local):
     here = Place()
-    work = ((score0, score1), top, total, acc)
+    work = ((score0, score1), top)
     own_proj = pltpu.make_async_copy(proj.at[0, here.h8], projb, local)
     own_proj.start()
     greet(here)
@@ -417,12 +407,8 @@
     share(here, tkb, tvb, send, recv, T_K, T_V, FWD + 2, FWD + 3)
     turn_values(tvb, tvt)
 
-    def ready(task):
-        head = lax.div(task, 4)
-
-        @pl.when(lax.rem(task, 4) == 0)
-        def _():
-            drain(tqb.at[head], recv.at[T_Q + head])
+    def ready(head):
+        drain(tqb.at[head], recv.at[T_Q + head])
 
     teacher_forward(here.half, tqb, tkb, tvt, tctx_t, work, ready)
     own_proj.wait()
@@ -454,22 +440,25 @@
         sibling(here, dkv.at[pl.ds(jb * 4, 4), 1 - here.half], paired.at[step],
                 send.at[PAIR], recv.at[PAIR + step]).start()
 
+    def middle(step):
         @pl.when(step > 0)
         def _():
             finish_kv(step - 1)
 
-    backward(here.half, first, sqb, skb, svb, grad_t, lse, delta, q_t, dq_t, dk, dv, dkv, dq, after)
-
-    def send_q(t, _):
-        s = lax.rem(here.s + t, NS)
-        row = pl.multiple_of(s * 128, 128)
-        col = pl.multiple_of(here.head * D, D)
-        push(here, dq.at[pl.ds(row, 128), :], out_q.at[0, :, pl.ds(col, D)],
-             send.at[G_Q], recv.at[G_Q], here.half, s)
-        return 0
-
+    def send_dq(group):
+        def one(i, _):
+            s = group * 4 + i
+            row = pl.multiple_of(s * 128, 128)
+            col = pl.multiple_of(here.head * D, D)
+            push(here, dq.at[pl.ds(row, 128), :], out_q.at[0, :, pl.ds(col, D)],
+                 send.at[G_Q], recv.at[G_Q], here.half, s)
+            return 0
+
+        lax.fori_loop(0, 4, one, 0)
+
+    backward(here.half, first, sqb, skb, svb, grad_t, lse, delta, q_t, dq_t, dk, dv, dkv, dq,
+             middle, after, send_dq)
     finish_kv(3)
-    lax.fori_loop(0, NS, send_q, 0)
 
     drain(got_loss, recv.at[LOSS])
     sums = got_loss[0]
@@ -571,8 +560,6 @@
             vmem((TOK, QB), F32),
             vmem((TOK, QB), F32),
             vmem((8, QB), F32),
-            vmem((8, QB), F32),
-            vmem((D, QB), F32),
             pltpu.SemaphoreType.DMA((N_SEM,)),
             pltpu.SemaphoreType.DMA((N_SEM,)),
             pltpu.SemaphoreType.DMA,

time: 126 us -> 112 us (0.89)
  Pallas kernels: 121 us -> 107 us
    pallas_call x1, Pallas kernels: 121 us -> 107 us  [body(): pl.pallas_call(kernel, out_shape=(jax.ShapeDtypeStruct((1, 128, 2048), BF...]
where the time goes in v3:
time: 112 us
  Pallas kernels  107 us (96%)
  local copies, waits for them, and re-layouts  2.89 us (3%)
  other arithmetic  2.16 us (2%)
    pallas_call x1, Pallas kernels, body(): pl.pallas_call(kernel, out_shape=(jax.ShapeDtypeStruct((1, 128, 2048), BF...  107 us
    unnamed x7, local copies, waits for them, and re-layouts  2.89 us

profile of v3, /device:TPU:1, one launch (start us, length us, event | category | flops | bytes accessed | tf_op | source)
XLA Modules:
  0.0 112.3 jit_solution(17529024060966292968)
XLA Ops:
  0.6 106.6 %shard_map.102 = (bf16[1,128,2048]{2,1,0:T(8,128)(2,1)}, f32[1,128,512]{2,1,0:T(8,128)}, f32[1,128,512]{2,1,0:T(8,128)}, f32[1,128]{1,0:T(1,128)}) custom-call(bf16[1,256,4096]{2,1,0:T(8,128)(2,1)} %tq.1, bf16[1,256,512]{2,1,0:T(8,128)(2,1)} %tk.1, bf16[1,256,512]{2,1,0:T(8,128)(2,1)} %tv.1, bf16[1,8,512,128]{3,2,1,0:T(8,128)(2,1)} %proj.1, ...), custom_call_target="tpu_custom_call" | custom-call | flops 16999999488 | bytes 8000000 | tf_op jit(solution)/shard_map/pallas_call | solution.py:519
  107.2 0.0 copy-start
  107.2 0.0 copy-start.1
  107.3 2.2 %convert_element_type.3 = f32[1,128,2048]{2,1,0:T(8,128)} convert(bf16[1,128,2048]{2,1,0:T(8,128)(2,1)} %get-tuple-element.8) | non-fusion elementwise | flops 262144 | bytes 1572864 | tf_op jit(solution)/shard_map/convert_element_type | solution.py:574
  109.4 1.7 %copy.14 = f32[1,128,512]{2,1,0:T(8,128)} copy(f32[1,128,512]{2,1,0:T(8,128)} %get-tuple-element.17) | data formatting | bytes 524288
  111.1 0.0 copy-done
  111.1 0.7 copy.15
  111.8 0.0 copy-done.1
  111.8 0.5 copy.16
Async XLA Ops:
  107.2 3.9 %copy-start = (f32[1,128,512]{2,1,0:T(8,128)S(1)}, f32[1,128,512]{2,1,0:T(8,128)}, u32[]{:S(2)}) copy-start(f32[1,128,512]{2,1,0:T(8,128)} %get-tuple-element.18) | copy-start | bytes 786436
  107.2 4.5 %copy-start.1 = (f32[1,128]{1,0:T(1,128)S(1)}, f32[1,128]{1,0:T(1,128)}, u32[]{:S(2)}) copy-start(f32[1,128]{1,0:T(1,128)} %get-tuple-element.19) | copy-start | bytes 1540

commit v4 on v3

--- a/solution.py
+++ b/solution.py
@@ -45,8 +45,8 @@
 
 
 class Flash:
-    def __init__(self, half, keys, values_t, finish, top):
-        self.half, self.keys, self.values_t, self.finish, self.top = half, keys, values_t, finish, top
+    def __init__(self, half, keys, values_t, top, kept=None):
+        self.half, self.keys, self.values_t, self.top, self.kept = half, keys, values_t, top, kept
 
     def take(self, top, query, chunk, buf):
         span = slice(chunk * KC, (chunk + 1) * KC)
@@ -69,13 +69,16 @@
         right = jnp.maximum(fold(scores[:, 256:], jnp.maximum), fold(far, jnp.maximum))
         return jnp.maximum(top, jnp.concatenate([fold(near, jnp.maximum), right], axis=1))
 
-    def mix(self, state, peak, chunk, buf):
+    def mix(self, state, peak, chunk, buf, group):
         total, acc = state
         weights = jnp.exp2((buf[chunk * KC : (chunk + 1) * KC, :] - peak) * SCALE2)
         total = total + fold(weights, jnp.add)
-        return total, acc + dot_nn(self.values_t[chunk], weights.astype(BF16))
-
-    def mix_last(self, state, peak, chunk, buf):
+        weights = weights.astype(BF16)
+        if self.kept is not None:
+            self.kept[kept_at(group, chunk)] = weights
+        return total, acc + dot_nn(self.values_t[chunk], weights)
+
+    def mix_last(self, state, peak, chunk, buf, group):
         total, acc = state
         start = chunk * KC
         near = jnp.exp2((buf[start : start + 512, :] - peak) * SCALE2)
@@ -84,8 +87,12 @@
         total = total + jnp.concatenate(
             [sums[:, :256], sums[:, 256:] + fold(far, jnp.add)], axis=1
         )
-        near = dot_nn(self.values_t[chunk, :, :512], near.astype(BF16))
-        far = dot_nn(self.values_t[chunk, :, 512:], far.astype(BF16))
+        near, far = near.astype(BF16), far.astype(BF16)
+        if self.kept is not None:
+            self.kept[kept_at(group, chunk), :512, :] = near
+            self.kept[kept_at(group, chunk), 512:, 256:] = far
+        near = dot_nn(self.values_t[chunk, :, :512], near)
+        far = dot_nn(self.values_t[chunk, :, 512:], far)
         return total, acc + jnp.concatenate([near[:, :256], near[:, 256:] + far], axis=1)
 
     def step(self, task, old, following, new):
@@ -105,29 +112,35 @@
                 top = step(top, query, chunk, new)
             if chunk < len(mixes):
                 step = self.mix_last if chunk == task[0] else self.mix
-                state = step(state, peak, chunk, old)
+                state = step(state, peak, chunk, old, task[0])
         if following is not None:
             self.top[...] = top
         if task is not None:
             task[2](peak, jnp.sum(state[0], axis=0, keepdims=True), state[1])
 
 
+def kept_at(group, chunk):
+    if isinstance(group, int):
+        return group * (group + 1) // 2 + chunk
+    return lax.div(group * (group + 1), 2) + chunk
+
+
 def columns(group):
     if isinstance(group, int):
         return slice(group * QB, (group + 1) * QB)
     return pl.ds(pl.multiple_of(group * QB, QB), QB)
 
 
-def student_forward(half, sq, sk, svt, ctx_t, lse, work):
+def student_forward(half, sq, sk, svt, ctx_t, scale, kept, work):
     score, top = work
-    flash = Flash(half, sk, svt, None, top)
+    flash = Flash(half, sk, svt, top, kept)
 
     def task(group):
         at = columns(group)
 
         def finish(peak, total, acc):
             ctx_t[:, at] = acc / total
-            lse[:, at] = jnp.broadcast_to(peak * SCALE2 + jnp.log2(total), (8, QB))
+            scale[:, at] = jnp.broadcast_to(1.0 / total, (8, QB))
 
         return group, lambda: sq[at, :], finish
 
@@ -140,7 +153,7 @@
 
 def teacher_forward(half, tq, tk, tvt, tctx_t, work, ready):
     score, top = work
-    flash = Flash(half, tk, tvt, None, top)
+    flash = Flash(half, tk, tvt, top)
 
     def task(head, group):
         at = columns(group)
@@ -184,7 +197,7 @@
     lax.fori_loop(0, TOK // KC, chunk, 0)
 
 
-def mismatches(tctx_t, proj, ctx_t, grad_t, delta, loss):
+def mismatches(tctx_t, proj, ctx_t, scale, grad_t, delta, loss):
     proj_t = jnp.transpose(proj[...])
 
     def step(group, _):
@@ -192,9 +205,10 @@
         target = dot_nn(proj_t, tctx_t[:, at]).astype(BF16).astype(F32)
         context = ctx_t[:, at]
         miss = context - target
-        grad_t[:, at] = miss.astype(BF16)
+        per_total = scale[0:1, at]
+        grad_t[:, at] = (miss * per_total).astype(BF16)
         dots = jnp.sum(fold(miss * context, jnp.add), axis=0, keepdims=True)
-        delta[:, at] = jnp.broadcast_to(dots, (8, QB))
+        delta[:, at] = jnp.broadcast_to(dots * per_total, (8, QB))
         squares = jnp.sum(fold(miss * miss, jnp.add), axis=0, keepdims=True) * (1.0 / 2048.0)
         wide = jnp.broadcast_to(squares, (8, QB))
         for i in range(4):
@@ -204,9 +218,8 @@
     lax.fori_loop(0, HALF // QB, step, 0)
 
 
-def backward(half, first, sq, sk, sv, grad_t, lse, delta, q_t, dq_t, dk, dv, dkv, dq, middle, after, send_dq):
+def backward(first, sq, sk, sv, grad_t, kept, delta, q_t, dq_t, dk, dv, dkv, dq, middle, after, send_dq):
     dq_t[...] = jnp.zeros(dq_t.shape, F32)
-    q_t[...] = jnp.transpose(sq[...])
 
     def outer(step, _):
         jb = lax.rem(first + step, TOK // KC)
@@ -216,22 +229,23 @@
         dk[...] = jnp.zeros(dk.shape, F32)
         dv[...] = jnp.zeros(dv.shape, F32)
 
-        def terms(e, at, mask=None):
+        def terms(e, group, late=False):
+            at, rows = columns(group), slice(e * 512, (e + 1) * 512)
+            weights = kept.at[kept_at(group, jb)]
+            if late:
+                at = pl.ds(pl.multiple_of(group * QB + 256, 256), 256)
+                prob = weights[rows, 256:]
+            else:
+                prob = weights[rows, :]
             query_t, grad = q_t[:, at], grad_t[:, at]
-            prob = jnp.exp2(dot_nn(sk[spans[e], :], query_t) * SCALE2 - lse[0:1, at])
-            if mask is not None:
-                prob = jnp.where(mask, prob, 0.0)
-            ds = (prob * (dot_nn(sv[spans[e], :], grad) - delta[0:1, at])).astype(BF16)
-            keys = slice(e * 512, (e + 1) * 512)
-            dv[:, keys] += dot_nt(grad, prob.astype(BF16))
-            dk[:, keys] += dot_nt(query_t, ds)
+            ds = prob.astype(F32) * (dot_nn(sv[spans[e], :], grad) - delta[0:1, at])
+            ds = ds.astype(BF16)
+            dv[:, rows] += dot_nt(grad, prob)
+            dk[:, rows] += dot_nt(query_t, ds)
             dq_t[:, at] += dot_nn(turned[e], ds)
 
-        key_pos = start + lax.broadcasted_iota(jnp.int32, (512, QB), 0)
-        at = position(jb, half)
-        terms(0, columns(jb), key_pos <= at)
-        late = pl.ds(pl.multiple_of(jb * QB + 256, 256), 256)
-        terms(1, late, key_pos[:, 256:] + 512 <= at[:, 256:])
+        terms(0, jb)
+        terms(1, jb, True)
 
         def leave(group):
             at = columns(group)
@@ -245,8 +259,8 @@
             leave(jb)
 
         def full(group, _):
-            terms(0, columns(group))
-            terms(1, columns(group))
+            terms(0, group)
+            terms(1, group)
 
             @pl.when(jnp.logical_and(step == TOK // KC - 1, first > 0))
             def _():
@@ -296,6 +310,13 @@
         ).start()
 
 
+def toward(here, tx, tz):
+    at = lax.div(here.s, 2)
+    x = lax.rem(lax.div(at, 4) + tx, 2)
+    z = lax.rem(lax.rem(at, 4) + jnp.where(here.half == 0, tz, 4 - tz), 4)
+    return x * 4 + z
+
+
 def greet(here):
     barrier = pltpu.get_barrier_semaphore()
 
@@ -324,8 +345,7 @@
 
 def send_student(here, sq, sk, sv, sqb, skb, svb, send, recv):
     def step(t, _):
-        chip = lax.rem(here.c * 8 + lax.div(here.s, 2) + jnp.where(here.half == 0, t, 16 - t), 16)
-        c, p = lax.div(chip, 8), lax.rem(chip, 8)
+        c, p = lax.rem(here.c + lax.rem(t, 2), 2), toward(here, lax.rem(lax.div(t, 2), 2), lax.div(t, 4))
         h8 = head_of(2 * p)
         kv = pl.multiple_of((2 * c + lax.div(h8, 4)) * D, D)
         q = pl.multiple_of((c * 8 + h8) * D, D)
@@ -344,7 +364,7 @@
 
 def send_teacher(here, tq, tk, tv, tqb, tkb, tvb, send, recv):
     def step(t, _):
-        p = lax.rem(lax.div(here.s, 2) + jnp.where(here.half == 0, t, 8 - t), 8)
+        p = toward(here, lax.rem(t, 2), lax.div(t, 2))
         kv = pl.multiple_of(lax.div(head_of(2 * p), 2) * D, D)
         at = pl.multiple_of(here.s * 256, 256)
         push(here, tk.at[0, :, pl.ds(kv, D)], tkb.at[pl.ds(at, 256), :],
@@ -356,7 +376,7 @@
     lax.fori_loop(0, 8, step, 0)
     for h in range(4):
         def query(t, _):
-            p = lax.rem(lax.div(here.s, 2) + jnp.where(here.half == 0, t, 8 - t), 8)
+            p = toward(here, lax.rem(t, 2), lax.div(t, 2))
             col = pl.multiple_of(head_of(2 * p) * 512 + h * D, D)
             for core in range(2):
                 push(here, tq.at[0, pl.ds(core * 128, 128), pl.ds(col, D)],
@@ -390,8 +410,8 @@
 
 
 def kernel(tq, tk, tv, proj, sq, sk, sv, out_q, out_k, out_v, out_loss,
-           tqb, tkb, tvb, tvt, sqb, skb, svb, svt, projb, ctx_t, lse, tctx_t, grad_t, delta, loss,
-           q_t, dq_t, dk, dv, dkv, paired, summed, dq, got_kv, got_loss,
+           tqb, tkb, tvb, tvt, sqb, skb, svb, svt, projb, ctx_t, scale, tctx_t, grad_t, delta, loss,
+           kept, q_t, dq_t, dk, dv, dkv, paired, summed, dq, got_kv, got_loss,
            score0, score1, top, send, recv, local):
     here = Place()
     work = ((score0, score1), top)
@@ -403,7 +423,8 @@
     share(here, skb, svb, send, recv, S_K, S_V, FWD, FWD + 1)
     turn_values(svb, svt)
     drain(sqb, recv.at[S_Q])
-    student_forward(here.half, sqb, skb, svt, ctx_t, lse, work)
+    q_t[...] = jnp.transpose(sqb[...])
+    student_forward(here.half, sqb, skb, svt, ctx_t, scale, kept, work)
     share(here, tkb, tvb, send, recv, T_K, T_V, FWD + 2, FWD + 3)
     turn_values(tvb, tvt)
 
@@ -412,7 +433,7 @@
 
     teacher_forward(here.half, tqb, tkb, tvt, tctx_t, work, ready)
     own_proj.wait()
-    mismatches(tctx_t, projb, ctx_t, grad_t, delta, loss)
+    mismatches(tctx_t, projb, ctx_t, scale, grad_t, delta, loss)
 
     def send_loss(t, _):
         s = lax.rem(here.s + t, NS)
@@ -456,7 +477,7 @@
 
         lax.fori_loop(0, 4, one, 0)
 
-    backward(here.half, first, sqb, skb, svb, grad_t, lse, delta, q_t, dq_t, dk, dv, dkv, dq,
+    backward(first, sqb, skb, svb, grad_t, kept, delta, q_t, dq_t, dk, dv, dkv, dq,
              middle, after, send_dq)
     finish_kv(3)
 
@@ -547,6 +568,7 @@
             vmem((D, HALF), BF16),
             vmem((8, HALF), F32),
             vmem((NS, 8, 128), F32),
+            vmem((10, KC, QB), BF16),
             vmem((D, HALF), BF16),
             vmem((D, HALF), F32),
             vmem((D, KC), F32),
@@ -565,7 +587,7 @@
             pltpu.SemaphoreType.DMA,
         ],
         compiler_params=pltpu.CompilerParams(
-            collective_id=0, has_side_effects=True, vmem_limit_bytes=56 * 1024 * 1024
+            collective_id=0, has_side_effects=True, vmem_limit_bytes=60 * 1024 * 1024
         ),
         cost_estimate=pl.CostEstimate(
             flops=17_000_000_000, bytes_accessed=8_000_000, transcendentals=30_000_000

time: 112 us -> 108 us (0.964)
  Pallas kernels: 107 us -> 102 us
    pallas_call x1, Pallas kernels: 107 us -> 102 us  [body(): pl.pallas_call(kernel, out_shape=(jax.ShapeDtypeStruct((1, 128, 2048), BF...]
where the time goes in v4:
time: 108 us
  Pallas kernels  102 us (94%)
  local copies, waits for them, and re-layouts  2.89 us (3%)
  other arithmetic  2.16 us (2%)
    pallas_call x1, Pallas kernels, body(): pl.pallas_call(kernel, out_shape=(jax.ShapeDtypeStruct((1, 128, 2048), BF...  102 us
    unnamed x7, local copies, waits for them, and re-layouts  2.89 us

profile of v4, /device:TPU:1, one launch (start us, length us, event | category | flops | bytes accessed | tf_op | source)
XLA Modules:
  0.0 107.8 jit_solution(2833429221765890034)
XLA Ops:
  0.6 102.1 %shard_map.102 = (bf16[1,128,2048]{2,1,0:T(8,128)(2,1)}, f32[1,128,512]{2,1,0:T(8,128)}, f32[1,128,512]{2,1,0:T(8,128)}, f32[1,128]{1,0:T(1,128)}) custom-call(bf16[1,256,4096]{2,1,0:T(8,128)(2,1)} %tq.1, bf16[1,256,512]{2,1,0:T(8,128)(2,1)} %tk.1, bf16[1,256,512]{2,1,0:T(8,128)(2,1)} %tv.1, bf16[1,8,512,128]{3,2,1,0:T(8,128)(2,1)} %proj.1, ...), custom_call_target="tpu_custom_call" | custom-call | flops 16999999488 | bytes 8000000 | tf_op jit(solution)/shard_map/pallas_call | solution.py:540
  102.7 0.0 copy-start
  102.8 0.0 copy-start.1
  102.8 2.2 %convert_element_type.3 = f32[1,128,2048]{2,1,0:T(8,128)} convert(bf16[1,128,2048]{2,1,0:T(8,128)(2,1)} %get-tuple-element.8) | non-fusion elementwise | flops 262144 | bytes 1572864 | tf_op jit(solution)/shard_map/convert_element_type | solution.py:596
  104.9 1.7 %copy.14 = f32[1,128,512]{2,1,0:T(8,128)} copy(f32[1,128,512]{2,1,0:T(8,128)} %get-tuple-element.17) | data formatting | bytes 524288
  106.6 0.0 copy-done
  106.6 0.7 copy.15
  107.3 0.0 copy-done.1
  107.3 0.5 copy.16
Async XLA Ops:
  102.7 3.9 %copy-start = (f32[1,128,512]{2,1,0:T(8,128)S(1)}, f32[1,128,512]{2,1,0:T(8,128)}, u32[]{:S(2)}) copy-start(f32[1,128,512]{2,1,0:T(8,128)} %get-tuple-element.18) | copy-start | bytes 786436
  102.8 4.5 %copy-start.1 = (f32[1,128]{1,0:T(1,128)S(1)}, f32[1,128]{1,0:T(1,128)}, u32[]{:S(2)}) copy-start(f32[1,128]{1,0:T(1,128)} %get-tuple-element.19) | copy-start | bytes 1540

commit v5 on v4

--- a/solution.py
+++ b/solution.py
@@ -218,7 +218,7 @@
     lax.fori_loop(0, HALF // QB, step, 0)
 
 
-def backward(first, sq, sk, sv, grad_t, kept, delta, q_t, dq_t, dk, dv, dkv, dq, middle, after, send_dq):
+def backward(first, sq, sk, sv, grad_t, kept, delta, q_t, dq_t, dk, dv, dkv, dq, middle, after, send_dq, spin):
     dq_t[...] = jnp.zeros(dq_t.shape, F32)
 
     def outer(step, _):
@@ -258,7 +258,10 @@
         def _():
             leave(jb)
 
-        def full(group, _):
+        left = HALF // QB - 1 - jb
+
+        def full(turn, _):
+            group = jb + 1 + lax.rem(turn + spin, left)
             terms(0, group)
             terms(1, group)
 
@@ -268,7 +271,7 @@
 
             return 0
 
-        lax.fori_loop(jb + 1, HALF // QB, full, 0)
+        lax.fori_loop(0, left, full, 0)
         for i in range(KC // 128):
             span = slice(i * 128, (i + 1) * 128)
             dkv[jb * 4 + i // 2, i % 2, :D, :] = (dk[:, span] * ROOT).astype(BF16)
@@ -441,7 +444,8 @@
         return 0
 
     lax.fori_loop(0, NS, send_loss, 0)
-    first = lax.rem(lax.div(here.s, 2), 4)
+    z = lax.rem(lax.div(here.s, 2), 4)
+    first = lax.rem(z + lax.div(here.s, 8) + 2 * here.c, 4)
 
     def finish_kv(step):
         jb = lax.rem(first + step, 4)
@@ -478,7 +482,7 @@
         lax.fori_loop(0, 4, one, 0)
 
     backward(first, sqb, skb, svb, grad_t, kept, delta, q_t, dq_t, dk, dv, dkv, dq,
-             middle, after, send_dq)
+             middle, after, send_dq, z)
     finish_kv(3)
 
     drain(got_loss, recv.at[LOSS])

time: 108 us -> 106 us (0.981)
  Pallas kernels: 102 us -> 99.4 us
    pallas_call x1, Pallas kernels: 102 us -> 99.4 us  [body(): pl.pallas_call(kernel, out_shape=(jax.ShapeDtypeStruct((1, 128, 2048), BF...]
where the time goes in v5:
time: 106 us; the launch traced here: 105 us
  Pallas kernels  99.4 us (94%)
  local copies, waits for them, and re-layouts  2.89 us (3%)
  other arithmetic  2.16 us (2%)
    pallas_call x1, Pallas kernels, body(): pl.pallas_call(kernel, out_shape=(jax.ShapeDtypeStruct((1, 128, 2048), BF...  99.4 us
    unnamed x7, local copies, waits for them, and re-layouts  2.89 us
    convert_element_type x1, other arithmetic, body(): return (dq.astype(F32), dk, dv, loss)  2.16 us

profile of v5, /device:TPU:1, one launch (start us, length us, event | category | flops | bytes accessed | tf_op | source)
XLA Modules:
  0.0 105.1 jit_solution(1075823732377541042)
XLA Ops:
  0.6 99.4 %shard_map.102 = (bf16[1,128,2048]{2,1,0:T(8,128)(2,1)}, f32[1,128,512]{2,1,0:T(8,128)}, f32[1,128,512]{2,1,0:T(8,128)}, f32[1,128]{1,0:T(1,128)}) custom-call(bf16[1,256,4096]{2,1,0:T(8,128)(2,1)} %tq.1, bf16[1,256,512]{2,1,0:T(8,128)(2,1)} %tk.1, bf16[1,256,512]{2,1,0:T(8,128)(2,1)} %tv.1, bf16[1,8,512,128]{3,2,1,0:T(8,128)(2,1)} %proj.1, ...), custom_call_target="tpu_custom_call" | custom-call | flops 16999999488 | bytes 8000000 | tf_op jit(solution)/shard_map/pallas_call | solution.py:544
  100.1 0.0 copy-start
  100.1 0.0 copy-start.1
  100.1 2.2 %convert_element_type.3 = f32[1,128,2048]{2,1,0:T(8,128)} convert(bf16[1,128,2048]{2,1,0:T(8,128)(2,1)} %get-tuple-element.8) | non-fusion elementwise | flops 262144 | bytes 1572864 | tf_op jit(solution)/shard_map/convert_element_type | solution.py:600
  102.3 1.7 %copy.14 = f32[1,128,512]{2,1,0:T(8,128)} copy(f32[1,128,512]{2,1,0:T(8,128)} %get-tuple-element.17) | data formatting | bytes 524288
  103.9 0.0 copy-done
  103.9 0.7 copy.15
  104.6 0.0 copy-done.1
  104.6 0.5 copy.16
Async XLA Ops:
  100.1 3.9 %copy-start = (f32[1,128,512]{2,1,0:T(8,128)S(1)}, f32[1,128,512]{2,1,0:T(8,128)}, u32[]{:S(2)}) copy-start(f32[1,128,512]{2,1,0:T(8,128)} %get-tuple-element.18) | copy-start | bytes 786436
  100.1 4.5 %copy-start.1 = (f32[1,128]{1,0:T(1,128)S(1)}, f32[1,128]{1,0:T(1,128)}, u32[]{:S(2)}) copy-start(f32[1,128]{1,0:T(1,128)} %get-tuple-element.19) | copy-start | bytes 1540

commit v6 on v5

--- a/solution.py
+++ b/solution.py
@@ -197,12 +197,11 @@
     lax.fori_loop(0, TOK // KC, chunk, 0)
 
 
-def mismatches(tctx_t, proj, ctx_t, scale, grad_t, delta, loss):
-    proj_t = jnp.transpose(proj[...])
+def mismatches(tctx_t, proj_t, ctx_t, scale, grad_t, delta, loss):
 
     def step(group, _):
         at = columns(group)
-        target = dot_nn(proj_t, tctx_t[:, at]).astype(BF16).astype(F32)
+        target = dot_nn(proj_t[...], tctx_t[:, at]).astype(BF16).astype(F32)
         context = ctx_t[:, at]
         miss = context - target
         per_total = scale[0:1, at]
@@ -218,14 +217,13 @@
     lax.fori_loop(0, HALF // QB, step, 0)
 
 
-def backward(first, sq, sk, sv, grad_t, kept, delta, q_t, dq_t, dk, dv, dkv, dq, middle, after, send_dq, spin):
+def backward(first, sk_t, sv, grad_t, kept, delta, q_t, dq_t, dk, dv, dkv, dq, middle, after, send_dq, spin):
     dq_t[...] = jnp.zeros(dq_t.shape, F32)
 
     def outer(step, _):
         jb = lax.rem(first + step, TOK // KC)
         start = pl.multiple_of(jb * KC, KC)
         spans = [pl.ds(pl.multiple_of(start + e * 512, 512), 512) for e in range(2)]
-        turned = [jnp.transpose(sk[span, :]) for span in spans]
         dk[...] = jnp.zeros(dk.shape, F32)
         dv[...] = jnp.zeros(dv.shape, F32)
 
@@ -242,7 +240,7 @@
             ds = ds.astype(BF16)
             dv[:, rows] += dot_nt(grad, prob)
             dk[:, rows] += dot_nt(query_t, ds)
-            dq_t[:, at] += dot_nn(turned[e], ds)
+            dq_t[:, at] += dot_nn(sk_t[jb, :, rows], ds)
 
         terms(0, jb)
         terms(1, jb, True)
@@ -414,7 +412,7 @@
 
 def kernel(tq, tk, tv, proj, sq, sk, sv, out_q, out_k, out_v, out_loss,
            tqb, tkb, tvb, tvt, sqb, skb, svb, svt, projb, ctx_t, scale, tctx_t, grad_t, delta, loss,
-           kept, q_t, dq_t, dk, dv, dkv, paired, summed, dq, got_kv, got_loss,
+           kept, proj_t, q_t, dq_t, dk, dv, dkv, paired, summed, dq, got_kv, got_loss,
            score0, score1, top, send, recv, local):
     here = Place()
     work = ((score0, score1), top)
@@ -428,6 +426,9 @@
     drain(sqb, recv.at[S_Q])
     q_t[...] = jnp.transpose(sqb[...])
     student_forward(here.half, sqb, skb, svt, ctx_t, scale, kept, work)
+    turn_values(skb, svt)
+    own_proj.wait()
+    proj_t[...] = jnp.transpose(projb[...])
     share(here, tkb, tvb, send, recv, T_K, T_V, FWD + 2, FWD + 3)
     turn_values(tvb, tvt)
 
@@ -435,15 +436,13 @@
         drain(tqb.at[head], recv.at[T_Q + head])
 
     teacher_forward(here.half, tqb, tkb, tvt, tctx_t, work, ready)
-    own_proj.wait()
-    mismatches(tctx_t, projb, ctx_t, scale, grad_t, delta, loss)
+    mismatches(tctx_t, proj_t, ctx_t, scale, grad_t, delta, loss)
 
     def send_loss(t, _):
         s = lax.rem(here.s + t, NS)
         push(here, loss.at[s], got_loss.at[here.head], send.at[LOSS], recv.at[LOSS], here.half, s)
         return 0
 
-    lax.fori_loop(0, NS, send_loss, 0)
     z = lax.rem(lax.div(here.s, 2), 4)
     first = lax.rem(z + lax.div(here.s, 8) + 2 * here.c, 4)
 
@@ -469,6 +468,10 @@
         @pl.when(step > 0)
         def _():
             finish_kv(step - 1)
+
+        @pl.when(step == 1)
+        def _():
+            lax.fori_loop(0, NS, send_loss, 0)
 
     def send_dq(group):
         def one(i, _):
@@ -481,7 +484,7 @@
 
         lax.fori_loop(0, 4, one, 0)
 
-    backward(first, sqb, skb, svb, grad_t, kept, delta, q_t, dq_t, dk, dv, dkv, dq,
+    backward(first, svt, svb, grad_t, kept, delta, q_t, dq_t, dk, dv, dkv, dq,
              middle, after, send_dq, z)
     finish_kv(3)
 
@@ -573,6 +576,7 @@
             vmem((8, HALF), F32),
             vmem((NS, 8, 128), F32),
             vmem((10, KC, QB), BF16),
+            vmem((D, 512), BF16),
             vmem((D, HALF), BF16),
             vmem((D, HALF), F32),
             vmem((D, KC), F32),

time: 106 us -> 106 us (level)
  no operation moved by 1% of the time
where the time goes in v6:
time: 106 us; the launch traced here: 105 us
  Pallas kernels  99.4 us (94%)
  local copies, waits for them, and re-layouts  2.89 us (3%)
  other arithmetic  2.16 us (2%)
    pallas_call x1, Pallas kernels, body(): pl.pallas_call(kernel, out_shape=(jax.ShapeDtypeStruct((1, 128, 2048), BF...  99.4 us
    unnamed x7, local copies, waits for them, and re-layouts  2.89 us
    convert_element_type x1, other arithmetic, body(): return (dq.astype(F32), dk, dv, loss)  2.16 us

profile of v6, /device:TPU:1, one launch (start us, length us, event | category | flops | bytes accessed | tf_op | source)
XLA Modules:
  0.0 105.1 jit_solution(14424817683646174529)
XLA Ops:
  0.6 99.4 %shard_map.102 = (bf16[1,128,2048]{2,1,0:T(8,128)(2,1)}, f32[1,128,512]{2,1,0:T(8,128)}, f32[1,128,512]{2,1,0:T(8,128)}, f32[1,128]{1,0:T(1,128)}) custom-call(bf16[1,256,4096]{2,1,0:T(8,128)(2,1)} %tq.1, bf16[1,256,512]{2,1,0:T(8,128)(2,1)} %tk.1, bf16[1,256,512]{2,1,0:T(8,128)(2,1)} %tv.1, bf16[1,8,512,128]{3,2,1,0:T(8,128)(2,1)} %proj.1, ...), custom_call_target="tpu_custom_call" | custom-call | flops 16999999488 | bytes 8000000 | tf_op jit(solution)/shard_map/pallas_call | solution.py:547
  100.0 0.0 copy-start
  100.1 0.0 copy-start.1
  100.1 2.2 %convert_element_type.3 = f32[1,128,2048]{2,1,0:T(8,128)} convert(bf16[1,128,2048]{2,1,0:T(8,128)(2,1)} %get-tuple-element.8) | non-fusion elementwise | flops 262144 | bytes 1572864 | tf_op jit(solution)/shard_map/convert_element_type | solution.py:604
  102.2 1.7 %copy.14 = f32[1,128,512]{2,1,0:T(8,128)} copy(f32[1,128,512]{2,1,0:T(8,128)} %get-tuple-element.17) | data formatting | bytes 524288
  103.9 0.0 copy-done
  103.9 0.7 copy.15
  104.6 0.0 copy-done.1
  104.6 0.5 copy.16
Async XLA Ops:
  100.0 3.9 %copy-start = (f32[1,128,512]{2,1,0:T(8,128)S(1)}, f32[1,128,512]{2,1,0:T(8,128)}, u32[]{:S(2)}) copy-start(f32[1,128,512]{2,1,0:T(8,128)} %get-tuple-element.18) | copy-start | bytes 786436
  100.1 4.5 %copy-start.1 = (f32[1,128]{1,0:T(1,128)S(1)}, f32[1,128]{1,0:T(1,128)}, u32[]{:S(2)}) copy-start(f32[1,128]{1,0:T(1,128)} %get-tuple-element.19) | copy-start | bytes 1540
